TPU v7x, 256 devices: a whole 4x4x8 slice. The times are simulated.
256 devices in a mesh: sp: 64 (over z, y, core), dp: 4 (over x).
Axes of the slice: x: 4, y: 4, z: 8, core: 2. Of those that a mesh axis runs over, the one named last changes fastest.
Arguments:
- queries: bfloat16 [32768, 8192], P(('dp', 'sp')), parts along dimension 0, may hold values from -60 to 60
- key_heads: bfloat16 [32768, 1024], P(('dp', 'sp')), parts along dimension 0, may hold values from -6 to 6
- value_heads: bfloat16 [32768, 1024], P(('dp', 'sp')), parts along dimension 0, may hold values from -6 to 6
- out_grad: bfloat16 [32768, 8192], P(('dp', 'sp')), parts along dimension 0, may hold values from -6 to 6
- segment_ids: int32 [32768], P(('dp', 'sp')), parts along dimension 0, may hold values from 0 to 31, never falling along the last dimension, each value on 1 to 512 neighbouring positions
Outputs:
- d_query: bfloat16 [32768, 8192], P(('dp', 'sp')), parts along dimension 0
- d_key: bfloat16 [32768, 1024], P(('dp', 'sp')), parts along dimension 0
- d_value: bfloat16 [32768, 1024], P(('dp', 'sp')), parts along dimension 0
There are 4 independent parts, one for each index of `dp`. A program takes and returns all parts, laid end to end along the dimension named above; each array names one. Nothing has to cross between parts.
Inputs may be any that keep to these rules, and one draw needn't show every extreme that they name: `segment_ids`: documents are runs of consecutive tokens with rising ids, each of at most 512 tokens; one has exactly 512.
All inputs are finite; a program needn't handle non-finite values.
Results may differ from a plain program's by a relative error of at most 0.0065.
Values may be sent and summed in bfloat16 or wider, within the bound.
No kernel may reach another device: no remote copies, remote signals or barrier semaphores. Data moves between devices by JAX's collectives and lax.ppermute only.
A program may use at most 192 MiB of HBM per device.

v0:
```python
import functools

import jax
import jax.numpy as jnp
from jax import lax
from jax.experimental import pallas as pl
from jax.experimental.pallas import tpu as pltpu
from jax.sharding import PartitionSpec as P

D = 128
T = 128
GROUP = 8
NEG = -1e30
CHUNKS = 2
CORE_HEADS = 4
HC = CORE_HEADS // CHUNKS
PAY = HC * 512 + 16
SMALL = 16 * 1024 * 1024
ROWS = 128
HALF = 512
SCALE = D ** -0.5
LOG2E = 1.4426950408889634
NT = (((1,), (1,)), ((), ()))
TN = (((0,), (0,)), ((), ()))
NN = (((1,), (0,)), ((), ()))
F32 = jnp.float32
BF16 = jnp.bfloat16


def rows(start, size, step=128):
    return pl.ds(pl.multiple_of(start, step), size)


def prep_kernel(info, key_in, value_in, ids_in, mine, theirs, key, value, ids, sems):
    c = info[0]
    pairs = ((key_in, key), (value_in, value), (ids_in, ids))
    copies = [pltpu.make_async_copy(a, b, sems.at[i]) for i, (a, b) in enumerate(pairs)]
    for copy in copies:
        copy.start()
    for copy in copies:
        copy.wait()
    for out, core in ((theirs, 1 - c), (mine, c)):
        for h in range(CORE_HEADS):
            cols = rows((core * CORE_HEADS + h) * D, D)
            out[(2 * h) * T:(2 * h + 1) * T, :] = key[:, cols]
            out[(2 * h + 1) * T:(2 * h + 2) * T, :] = value[:, cols]
        out[2 * CORE_HEADS * T:, :] = jnp.broadcast_to(ids[...].astype(F32), (16, T)).astype(BF16)


def join_kernel(info, mine, other, *outs):
    c = info[0]
    for j, out in enumerate(outs):
        for ht in range(2 * HC):
            src = (j * 2 * HC + ht) * T
            out[rows(ht * 256 + c * T, T), :] = mine[src:src + T, :]
            out[rows(ht * 256 + (1 - c) * T, T), :] = other[src:src + T, :]
        a = mine[2 * CORE_HEADS * T:, :].astype(F32)
        b = other[2 * CORE_HEADS * T:, :].astype(F32)
        row = lax.broadcasted_iota(jnp.int32, (16, T), 0)
        out[HC * 512:, :] = jnp.where(row == c, a, b).astype(BF16)


def load_ids(info, idrow, kvo, kv1, kv2):
    ids = slice(HC * 512, HC * 512 + 2)
    idrow[0:2, :] = jnp.where(info[1] >= 2, kv2[ids, :].astype(F32), -1.0)
    idrow[2:4, :] = jnp.where(info[1] >= 1, kv1[ids, :].astype(F32), -1.0)
    idrow[4:6, :] = kvo[ids, :].astype(F32)


def first_id(idrow, s):
    mine = idrow[pl.ds(s + 4, 1), :]
    return jnp.max(jnp.where(lax.broadcasted_iota(jnp.int32, (1, T), 1) == 0, mine, -2.0))


def block_count(idrow, s):
    count = jnp.int32(1)
    for b in range(4):
        same = jnp.max(idrow[pl.ds(s + b, 1), :]) == first_id(idrow, s)
        count = count + same.astype(jnp.int32)
    return count


def main_kernel(chunk, info, kvo, kv1, kv2, qs, gs, own, out1, out2, ds,
                idrow, nb, bias, kwin, vwin, acc_k, acc_v, ps, es, dps):
    base = chunk * HC
    c = info[0]
    load_ids(info, idrow, kvo, kv1, kv2)
    key_at = lax.broadcasted_iota(jnp.int32, (T, T), 0)
    query_at = lax.broadcasted_iota(jnp.int32, (T, T), 1)
    for n in range(2):
        s = c if n == 0 else 1 - c
        mine = idrow[pl.ds(s + 4, 1), :]
        for b in range(5):
            keys = idrow[pl.ds(s + b, 1), :]
            same = jnp.transpose(jnp.broadcast_to(keys, (T, T))) == mine
            if b == 4:
                same = same & (key_at <= query_at)
            bias[n, b * T:(b + 1) * T, :] = jnp.where(same, 0.0, NEG)
        nb[n] = block_count(idrow, s)

    def window(h, n, off, blocks):
        width = blocks * T
        skip = 640 - width
        at = rows(off + skip, width)
        kw, vw = kwin[at, :], vwin[at, :]
        b1 = bias[n, skip:, :]
        b2 = jnp.concatenate([b1, b1], axis=1)
        row = (base + h) * 1024
        for pair in range(GROUP // 2):
            cols = slice(pair * 256, (pair + 1) * 256)
            of_pair = rows(row + pair * 256, 256)
            score = lax.dot_general(kw, qs[n, of_pair, :], NT, preferred_element_type=F32)
            dp = lax.dot_general(vw, gs[n, of_pair, :], NT, preferred_element_type=F32)
            stats = []
            for b in range(0, width, ROWS):
                x = score[b:b + ROWS] * (SCALE * LOG2E) + b2[b:b + ROWS]
                x = x.reshape(ROWS // 8, 8, 256)
                y = dp[b:b + ROWS].reshape(ROWS // 8, 8, 256)
                top = jnp.max(x, axis=0)
                e = jnp.exp2(x - top)
                stats.append((top, jnp.sum(e, axis=0), jnp.sum(e * y, axis=0)))
                es[pair % 2, b:b + ROWS, :] = e.reshape(ROWS, 256)
                dps[pair % 2, b:b + ROWS, :] = dp[b:b + ROWS]
            top = stats[0][0]
            for t, _, _ in stats[1:]:
                top = jnp.maximum(top, t)
            top = jnp.max(top, axis=0, keepdims=True)
            fs = [jnp.exp2(t - top) for t, _, _ in stats]
            total = sum(f * l for f, (_, l, _) in zip(fs, stats))
            inv = 1.0 / jnp.sum(total, axis=0, keepdims=True)
            total = sum(f * d for f, (_, _, d) in zip(fs, stats))
            delta = jnp.sum(total, axis=0, keepdims=True) * inv
            for b, f in zip(range(0, width, ROWS), fs):
                at_b = slice(b, b + ROWS)
                p = es[pair % 2, at_b, :].reshape(ROWS // 8, 8, 256) * (f * inv)
                y = dps[pair % 2, at_b, :].reshape(ROWS // 8, 8, 256)
                ps[at_b, cols] = p.reshape(ROWS, 256).astype(BF16)
                ds[h, n, skip + b:skip + b + ROWS, cols] = (p * (y - delta)).reshape(ROWS, 256).astype(BF16)
            done = (pair + 1) * 256
            if done % HALF == 0:
                part = slice(done - HALF, done)
                of_part = rows(row + done - HALF, HALF)
                acc_v[at, :] += lax.dot_general(
                    ps[0:width, part], gs[n, of_part, :], NN, preferred_element_type=F32)
                acc_k[at, :] += lax.dot_general(
                    ds[h, n, skip:, part], qs[n, of_part, :], NN, preferred_element_type=F32)

    def one_head(h, carry):
        for at, ref in ((0, kv2), (256, kv1), (512, kvo)):
            kwin[at:at + 256, :] = ref[rows(h * 512, 256), :]
            vwin[at:at + 256, :] = ref[rows(h * 512 + 256, 256), :]
        acc_k[...] = jnp.zeros_like(acc_k)
        acc_v[...] = jnp.zeros_like(acc_v)

        def half(n, carry):
            off = jnp.where(n == 0, c, 1 - c) * T
            for blocks in range(1, 6):
                @pl.when(nb[n] == blocks)
                def _():
                    window(h, n, off, blocks)
            return carry

        lax.fori_loop(0, 2, half, 0)
        for at, ref in ((0, out2), (256, out1), (512, own)):
            ref[rows(h * 512, 256), :] = (acc_k[at:at + 256, :] * SCALE).astype(ref.dtype)
            ref[rows(h * 512 + 256, 256), :] = acc_v[at:at + 256, :].astype(ref.dtype)
        return carry

    lax.fori_loop(0, HC, one_head, 0)


def query_kernel(info, *refs):
    c = info[0]
    ins, (dqo, dqr, idrow, nb, kwin, dqs) = refs[:4 * CHUNKS], refs[4 * CHUNKS:]
    load_ids(info, idrow, *ins[:3])
    for n in range(2):
        nb[n] = block_count(idrow, c if n == 0 else 1 - c)
    for j in range(CHUNKS):
        kvo, kv1, kv2, ds = ins[4 * j:4 * j + 4]

        def one_head(h, carry):
            for at, ref in ((0, kv2), (256, kv1), (512, kvo)):
                kwin[at:at + 256, :] = ref[rows(h * 512, 256), :]
            col = (j * HC + h) * (GROUP * D)
            for n, out in enumerate((dqo, dqr)):
                off = (c if n == 0 else 1 - c) * T
                for blocks in range(1, 6):
                    @pl.when(nb[n] == blocks)
                    def _():
                        skip = 640 - blocks * T
                        kw = kwin[rows(off + skip, blocks * T), :]
                        dqs[...] = (lax.dot_general(
                            ds[h, n, skip:, :], kw, TN, preferred_element_type=F32) * SCALE
                        ).astype(BF16)
                for i in range(GROUP):
                    out[:, rows(col + i * D, D)] = dqs[i * T:(i + 1) * T, :]
            return carry

        lax.fori_loop(0, HC, one_head, 0)


def stage_kernel(info, query, grad, query_other, grad_other, qs, gs):
    start = info[0] * (CORE_HEADS * GROUP * D)
    for n, parts in enumerate(((query, grad), (query_other, grad_other))):
        for part, out in zip(parts, (qs, gs)):
            for i in range(CORE_HEADS * GROUP):
                out[n, i * T:(i + 1) * T, :] = part[:, rows(start + i * D, D)]


def place_kernel(info, mine, other, after, out, token):
    c = info[0]
    width = CORE_HEADS * GROUP * D
    for part, core in ((mine, c), (other, 1 - c)):
        for i in range(0, width, D):
            out[:, rows(core * width + i, D)] = part[:, i:i + D]
    token[...] = jnp.zeros_like(token)


def sum_kernel(info, own, b1, b2, mine, theirs):
    c = info[0]
    for out, core in ((mine, c), (theirs, 1 - c)):
        for ht in range(2 * HC):
            at = rows(ht * 256 + core * T, T)
            out[ht * T:(ht + 1) * T, :] = (
                own[at, :] + b1[at, :].astype(F32) + b2[at, :].astype(F32)).astype(BF16)


def last_kernel(info, *refs):
    c = info[0]
    mine, other, (key, value) = refs[:CHUNKS], refs[CHUNKS:2 * CHUNKS], refs[2 * CHUNKS + 1:]
    for part, core in ((mine, c), (other, 1 - c)):
        for j in range(CHUNKS):
            for h in range(HC):
                cols = rows((core * CORE_HEADS + j * HC + h) * D, D)
                key[:, cols] = part[j][(2 * h) * T:(2 * h + 1) * T, :]
                value[:, cols] = part[j][(2 * h + 1) * T:(2 * h + 2) * T, :]


def shape(*dims, dtype=BF16):
    return jax.ShapeDtypeStruct(dims, dtype)


SMEM = pl.BlockSpec(memory_space=pltpu.SMEM)
ANY = pl.BlockSpec(memory_space=pl.ANY)
HBM = pl.BlockSpec(memory_space=pltpu.HBM)
FREE = pl.CostEstimate(flops=0, bytes_accessed=0, transcendentals=0)
MID = pl.CostEstimate(flops=2 * 10 ** 10, bytes_accessed=0, transcendentals=0)
LONG = pl.CostEstimate(flops=10 ** 11, bytes_accessed=10 ** 8, transcendentals=0)
VMEM = pl.BlockSpec(memory_space=pltpu.VMEM)


def simple(kernel, outs, count, flops=0):
    return pl.pallas_call(
        kernel,
        out_shape=outs,
        in_specs=[SMEM] + [VMEM] * count,
        out_specs=tuple(VMEM for _ in outs),
        compiler_params=pltpu.CompilerParams(vmem_limit_bytes=SMALL),
            cost_estimate=FREE,
    )


def main_call(chunk, info, payload, r1, r2, qs, gs):
    return pl.pallas_call(
        functools.partial(main_kernel, chunk),
        in_specs=[SMEM] + [VMEM] * 5,
        out_specs=[VMEM] * 4,
        scratch_shapes=[
            pltpu.VMEM((8, T), F32),
            pltpu.SMEM((2,), jnp.int32),
            pltpu.VMEM((2, 640, T), F32),
            pltpu.VMEM((768, D), BF16),
            pltpu.VMEM((768, D), BF16),
            pltpu.VMEM((768, D), F32),
            pltpu.VMEM((768, D), F32),
            pltpu.VMEM((640, 1024), BF16),
            pltpu.VMEM((2, 640, 256), F32),
            pltpu.VMEM((2, 640, 256), F32),
        ],
        out_shape=[
            shape(HC * 512, T, dtype=F32),
            shape(HC * 512, T),
            shape(HC * 512, T),
            shape(HC, 2, 640, 1024),
        ],
        compiler_params=pltpu.CompilerParams(vmem_limit_bytes=24 * 1024 * 1024),
        cost_estimate=LONG,
    )(info, payload, r1, r2, qs, gs)


def body(queries, key_heads, value_heads, out_grad, segment_ids):
    devices = lax.axis_size("sp")
    me = lax.axis_index("sp")
    c, k = me % 2, me // 2
    info = jnp.stack([c, k]).astype(jnp.int32)
    swap = [(i, i ^ 1) for i in range(devices)]

    def ring(by):
        return [(i, (i + by) % devices) for i in range(devices)]

    def send(x, perm):
        return lax.ppermute(x, "sp", perm)

    side = shape(2 * CORE_HEADS * T + 16, T)
    kv_in = pltpu.VMEM((T, 2 * CORE_HEADS * D), BF16)
    mine, theirs = pl.pallas_call(
        prep_kernel,
        out_shape=(side, side),
        in_specs=[SMEM, HBM, HBM, HBM],
        out_specs=(VMEM, VMEM),
        scratch_shapes=[
            kv_in, kv_in, pltpu.VMEM((1, T), jnp.int32), pltpu.SemaphoreType.DMA((3,))],
        compiler_params=pltpu.CompilerParams(vmem_limit_bytes=SMALL),
        cost_estimate=FREE,
    )(info, key_heads, value_heads, segment_ids.reshape(1, T))
    other = send(theirs, swap)
    q_late, g_late, other = lax.optimization_barrier((queries, out_grad, other))
    q_other, g_other = send(q_late, swap), send(g_late, swap)
    payloads = simple(join_kernel, (shape(PAY, T),) * CHUNKS, 2)(info, mine, other)
    near, far = send(payloads[0], ring(2)), send(payloads[0], ring(4))
    stacked = shape(2, CORE_HEADS * GROUP * T, D)
    qs, gs = simple(stage_kernel, (stacked, stacked), 4)(info, queries, out_grad, q_other, g_other)
    rest, qs, gs = lax.optimization_barrier((payloads[1:], qs, gs))
    came = [(near, far)]
    came += [(send(p, ring(2)), send(p, ring(4))) for p in rest]

    sums, score_grads, kv_mine, kv_other = [], [], [], []
    for j in range(CHUNKS):
        own, out1, out2, ds = main_call(j, info, payloads[j], *came[j], qs, gs)
        if sums:
            own_a, near_a, far_a = sums[-1]
            out1, out2, ds, near_a = lax.optimization_barrier((out1, out2, ds, near_a))
            sums[-1] = own_a, near_a, far_a
        b2 = send(out2, ring(-4))
        b1 = send(out1, ring(-2))
        sums.append((own, b1, b2))
        score_grads += [payloads[j], *came[j], ds]
    half = shape(T, CORE_HEADS * GROUP * D)
    dq_mine, dq_send = pl.pallas_call(
        query_kernel,
        out_shape=(half, half),
        in_specs=[SMEM] + [VMEM] * (4 * CHUNKS),
        out_specs=(VMEM, VMEM),
        scratch_shapes=[
            pltpu.VMEM((8, T), F32),
            pltpu.SMEM((2,), jnp.int32),
            pltpu.VMEM((768, D), BF16),
            pltpu.VMEM((1024, D), BF16),
        ],
        compiler_params=pltpu.CompilerParams(vmem_limit_bytes=SMALL),
        cost_estimate=LONG,
    )(info, *score_grads)
    dq_other = send(dq_send, swap)
    half = shape(2 * HC * T, T)
    for j in range(CHUNKS):
        a, b = pl.pallas_call(
            sum_kernel,
            out_shape=(half, half),
            in_specs=[SMEM, VMEM, VMEM, VMEM],
            out_specs=(VMEM, VMEM),
            compiler_params=pltpu.CompilerParams(vmem_limit_bytes=SMALL),
            cost_estimate=MID if j == CHUNKS - 1 else FREE,
        )(info, *sums[j])
        kv_mine.append(a)
        kv_other.append(send(b, swap))
    d_query, token = pl.pallas_call(
        place_kernel,
        out_shape=(shape(T, 2 * CORE_HEADS * GROUP * D), shape(8, T, dtype=F32)),
        in_specs=[SMEM, VMEM, VMEM, ANY],
        out_specs=(VMEM, VMEM),
        compiler_params=pltpu.CompilerParams(vmem_limit_bytes=SMALL),
        cost_estimate=FREE,
    )(info, dq_mine, dq_other, kv_mine[-1])
    out = shape(T, 2 * CORE_HEADS * D)
    d_key, d_value = pl.pallas_call(
        last_kernel,
        out_shape=(out, out),
        in_specs=[SMEM] + [VMEM] * (2 * CHUNKS) + [ANY],
        out_specs=(VMEM, VMEM),
        compiler_params=pltpu.CompilerParams(vmem_limit_bytes=SMALL),
            cost_estimate=FREE,
    )(info, *kv_mine, *kv_other, token)
    return (d_query, d_key, d_value)


def solution(mesh):
    row = P(("dp", "sp"), None)
    return jax.shard_map(
        body,
        mesh=mesh,
        in_specs=(row, row, row, row, P(("dp", "sp"))),
        out_specs=(row, row, row),
        check_vma=False,
    )
```

profile of v0, /device:TPU:151, one launch (start us, length us, event | category | flops | bytes accessed | tf_op | source)
XLA Modules:
  0.0 71.0 jit_solution(13136968307164267450)
XLA Ops:
  0.6 0.1 pad_add_fusion.info
  0.7 0.0 copy-start.2
  0.7 0.9 %copy-done.2 = bf16[128,1024]{1,0:T(8,128)(2,1)S(1)} copy-done((bf16[128,1024]{1,0:T(8,128)(2,1)S(1)}, bf16[128,1024]{1,0:T(8,128)(2,1)}, u32[]{:S(2)}) %copy-start.2) | copy-done | bytes 262168
  1.7 0.0 copy-start.3
  1.7 0.9 %copy-done.3 = bf16[128,1024]{1,0:T(8,128)(2,1)S(1)} copy-done((bf16[128,1024]{1,0:T(8,128)(2,1)S(1)}, bf16[128,1024]{1,0:T(8,128)(2,1)}, u32[]{:S(2)}) %copy-start.3) | copy-done | bytes 262168
  2.6 0.0 copy-start.4
  2.6 0.7 copy-done.4
  3.3 0.7 %shard_map.76 = (bf16[1040,128]{1,0:T(8,128)(2,1)S(1)}, bf16[1040,128]{1,0:T(8,128)(2,1)S(1)}) custom-call(s32[2]{0:T(128)S(1)} %pad_add_fusion.info, bf16[128,1024]{1,0:T(8,128)(2,1)S(1)} %copy-done.2, bf16[128,1024]{1,0:T(8,128)(2,1)S(1)} %copy-done.3, s32[1,128]{1,0:T(1,128)S(1)} %bitcast.3), custom_call_target="tpu_custom_call" | custom-call | tf_op jit(solution)/shard_map/pallas_call | solution.py:306
  4.0 0.8 %collective-permute-start = (bf16[1040,128]{1,0:T(8,128)(2,1)S(1)}, bf16[1040,128]{1,0:T(8,128)(2,1)S(1)}, u32[]{:S(2)}, u32[]{:S(2)}) collective-permute-start(bf16[1040,128]{1,0:T(8,128)(2,1)S(1)} %get-tuple-element.38), channel_id=1, source_target_pairs={{0,4},{4,0},{8,12},{12,8},{16,20},{20,16},{24,28},{28,24},{32,36},... | collective-permute-start | bytes 798728 | tf_op jit(solution)/shard_map/ppermute | solution.py:302
  4.8 1.2 %collective-permute-done.other = bf16[1040,128]{1,0:T(8,128)(2,1)S(1)} collective-permute-done((bf16[1040,128]{1,0:T(8,128)(2,1)S(1)}, bf16[1040,128]{1,0:T(8,128)(2,1)S(1)}, u32[]{:S(2)}, u32[]{:S(2)}) %collective-permute-start) | collective-permute-done | bytes 266272 | tf_op jit(solution)/shard_map/ppermute | solution.py:302
  6.0 0.4 collective-permute-start.3
  6.3 0.1 collective-permute-start.4
  6.5 0.6 shard_map.77
  7.1 0.6 collective-permute-start.2
  7.7 1.9 %collective-permute-start.1 = (bf16[1040,128]{1,0:T(8,128)(2,1)S(1)}, bf16[1040,128]{1,0:T(8,128)(2,1)S(1)}, u32[]{:S(2)}, u32[]{:S(2)}) collective-permute-start(bf16[1040,128]{1,0:T(8,128)(2,1)S(1)} %get-tuple-element.40.kvo.refs_0_), channel_id=1, source_target_pairs={{0,8},{4,12},{8,16},{12,20},{16,24},{20,28},{24,32},{28,36},{32,40... | collective-permute-start | bytes 798728 | tf_op jit(solution)/shard_map/ppermute | solution.py:302
  9.6 0.8 %collective-permute-done.3.query_other = bf16[128,8192]{1,0:T(8,128)(2,1)S(1)} collective-permute-done((bf16[128,8192]{1,0:T(8,128)(2,1)}, bf16[128,8192]{1,0:T(8,128)(2,1)S(1)}, u32[]{:S(2)}, u32[]{:S(2)}) %collective-permute-start.3) | collective-permute-done | bytes 2097184 | tf_op jit(solution)/shard_map/ppermute | solution.py:302
  10.3 3.0 %collective-permute-done.4.grad_other = bf16[128,8192]{1,0:T(8,128)(2,1)S(1)} collective-permute-done((bf16[128,8192]{1,0:T(8,128)(2,1)}, bf16[128,8192]{1,0:T(8,128)(2,1)S(1)}, u32[]{:S(2)}, u32[]{:S(2)}) %collective-permute-start.4) | collective-permute-done | bytes 2097184 | tf_op jit(solution)/shard_map/ppermute | solution.py:302
  13.3 0.0 copy-start
  13.3 1.6 %copy-done = bf16[128,8192]{1,0:T(8,128)(2,1)S(1)} copy-done((bf16[128,8192]{1,0:T(8,128)(2,1)S(1)}, bf16[128,8192]{1,0:T(8,128)(2,1)}, u32[]{:S(2)}) %copy-start) | copy-done | bytes 2097176
  14.9 0.0 copy-start.1
  14.9 1.6 %copy-done.1 = bf16[128,8192]{1,0:T(8,128)(2,1)S(1)} copy-done((bf16[128,8192]{1,0:T(8,128)(2,1)S(1)}, bf16[128,8192]{1,0:T(8,128)(2,1)}, u32[]{:S(2)}) %copy-start.1) | copy-done | bytes 2097176
  16.5 1.6 %shard_map.78 = (bf16[2,4096,128]{2,1,0:T(8,128)(2,1)S(1)}, bf16[2,4096,128]{2,1,0:T(8,128)(2,1)S(1)}) custom-call(s32[2]{0:T(128)S(1)} %pad_add_fusion.info, bf16[128,8192]{1,0:T(8,128)(2,1)S(1)} %copy-done, bf16[128,8192]{1,0:T(8,128)(2,1)S(1)} %copy-done.1, bf16[128,8192]{1,0:T(8,128)(2,1)S(1)} %collective-permute-done.3.query_other, ...), custom_call_target="tpu_custom_call" | custom-call | tf_op jit(solution)/shard_map/pallas_call | solution.py:322
  18.2 0.6 collective-permute-start.6
  18.7 1.9 %collective-permute-start.5 = (bf16[1040,128]{1,0:T(8,128)(2,1)S(1)}, bf16[1040,128]{1,0:T(8,128)(2,1)S(1)}, u32[]{:S(2)}, u32[]{:S(2)}) collective-permute-start(bf16[1040,128]{1,0:T(8,128)(2,1)S(1)} %get-tuple-element.49.kvo.refs_4_), channel_id=1, source_target_pairs={{0,8},{4,12},{8,16},{12,20},{16,24},{20,28},{24,32},{28,36},{32,40... | collective-permute-start | bytes 798728 | tf_op jit(solution)/shard_map/ppermute | solution.py:302
  20.6 0.0 collective-permute-done.2.kv2.refs_2_
  20.6 0.5 collective-permute-done.1.kv1.refs_1_
  21.1 6.4 %shard_map.79 = (f32[1024,128]{1,0:T(8,128)S(1)}, bf16[1024,128]{1,0:T(8,128)(2,1)S(1)}, bf16[1024,128]{1,0:T(8,128)(2,1)S(1)}, bf16[2,2,640,1024]{3,2,1,0:T(8,128)(2,1)S(1)}) custom-call(s32[2]{0:T(128)S(1)} %pad_add_fusion.info, bf16[1040,128]{1,0:T(8,128)(2,1)S(1)} %get-tuple-element.40.kvo.refs_0_, ...), custom_call_target="tpu_custom_call" | custom-call | flops 99999997952 | bytes 100000000 | tf_op jit(solution)/shard_map/pallas_call | solution.py:264
  27.5 1.3 %collective-permute-start.7 = (bf16[1024,128]{1,0:T(8,128)(2,1)S(1)}, bf16[1024,128]{1,0:T(8,128)(2,1)S(1)}, u32[]{:S(2)}, u32[]{:S(2)}) collective-permute-start(bf16[1024,128]{1,0:T(8,128)(2,1)S(1)} %get-tuple-element.53), channel_id=1, source_target_pairs={{0,248},{4,252},{8,0},{12,4},{16,8},{20,12},{24,16},{28,20},{32,24... | collective-permute-start | bytes 786440 | tf_op jit(solution)/shard_map/ppermute | solution.py:302
  28.7 4.9 %collective-permute-start.11 = (bf16[1024,128]{1,0:T(8,128)(2,1)S(1)}, bf16[1024,128]{1,0:T(8,128)(2,1)S(1)}, u32[]{:S(2)}, u32[]{:S(2)}) collective-permute-start(bf16[1024,128]{1,0:T(8,128)(2,1)S(1)} %get-tuple-element.64), channel_id=1, source_target_pairs={{0,240},{4,244},{8,248},{12,252},{16,0},{20,4},{24,8},{28,12},{32,... | collective-permute-start | bytes 786440 | tf_op jit(solution)/shard_map/ppermute | solution.py:302
  33.6 0.0 collective-permute-done.6.kv2.refs_6_
  33.6 0.0 collective-permute-done.5.kv1.refs_5_
  33.6 6.4 %shard_map.80 = (f32[1024,128]{1,0:T(8,128)S(1)}, bf16[1024,128]{1,0:T(8,128)(2,1)S(1)}, bf16[1024,128]{1,0:T(8,128)(2,1)S(1)}, bf16[2,2,640,1024]{3,2,1,0:T(8,128)(2,1)S(1)}) custom-call(s32[2]{0:T(128)S(1)} %pad_add_fusion.info, bf16[1040,128]{1,0:T(8,128)(2,1)S(1)} %get-tuple-element.49.kvo.refs_4_, ...), custom_call_target="tpu_custom_call" | custom-call | flops 99999997952 | bytes 100000000 | tf_op jit(solution)/shard_map/pallas_call | solution.py:264
  40.0 0.0 collective-permute-done.7.b1
  40.0 0.6 collective-permute-start.9
  40.6 6.0 %collective-permute-start.10 = (bf16[1024,128]{1,0:T(8,128)(2,1)S(1)}, bf16[1024,128]{1,0:T(8,128)(2,1)S(1)}, u32[]{:S(2)}, u32[]{:S(2)}) collective-permute-start(bf16[1024,128]{1,0:T(8,128)(2,1)S(1)} %get-tuple-element.59), channel_id=1, source_target_pairs={{0,240},{4,244},{8,248},{12,252},{16,0},{20,4},{24,8},{28,12},{32,... | collective-permute-start | bytes 786440 | tf_op jit(solution)/shard_map/ppermute | solution.py:302
  46.6 4.2 %collective-permute-done.11.b2 = bf16[1024,128]{1,0:T(8,128)(2,1)S(1)} collective-permute-done((bf16[1024,128]{1,0:T(8,128)(2,1)S(1)}, bf16[1024,128]{1,0:T(8,128)(2,1)S(1)}, u32[]{:S(2)}, u32[]{:S(2)}) %collective-permute-start.11) | collective-permute-done | bytes 262176 | tf_op jit(solution)/shard_map/ppermute | solution.py:302
  50.7 0.6 shard_map.84
  51.4 3.3 %collective-permute-start.12 = (bf16[512,128]{1,0:T(8,128)(2,1)S(1)}, bf16[512,128]{1,0:T(8,128)(2,1)S(1)}, u32[]{:S(2)}, u32[]{:S(2)}) collective-permute-start(bf16[512,128]{1,0:T(8,128)(2,1)S(1)} %get-tuple-element.66), channel_id=1, source_target_pairs={{0,4},{4,0},{8,12},{12,8},{16,20},{20,16},{24,28},{28,24},{32,36},... | collective-permute-start | bytes 393224 | tf_op jit(solution)/shard_map/ppermute | solution.py:302
  54.7 4.6 %shard_map.81 = (bf16[128,4096]{1,0:T(8,128)(2,1)S(1)}, bf16[128,4096]{1,0:T(8,128)(2,1)S(1)}) custom-call(s32[2]{0:T(128)S(1)} %pad_add_fusion.info, bf16[1040,128]{1,0:T(8,128)(2,1)S(1)} %get-tuple-element.40.kvo.refs_0_, bf16[1040,128]{1,0:T(8,128)(2,1)S(1)} %collective-permute-done.1.kv1.refs_1_, ...), custom_call_target="tpu_custom_call" | custom-call | flops 99999997952 | bytes 100000000 | tf_op jit(solution)/shard_map/pallas_call | solution.py:339
  59.2 0.1 collective-permute-start.8
  59.3 0.0 collective-permute-done.9.b1
  59.4 4.8 %collective-permute-done.10.b2 = bf16[1024,128]{1,0:T(8,128)(2,1)S(1)} collective-permute-done((bf16[1024,128]{1,0:T(8,128)(2,1)S(1)}, bf16[1024,128]{1,0:T(8,128)(2,1)S(1)}, u32[]{:S(2)}, u32[]{:S(2)}) %collective-permute-start.10) | collective-permute-done | bytes 262176 | tf_op jit(solution)/shard_map/ppermute | solution.py:302
  64.1 0.6 shard_map.82
  64.8 2.4 %collective-permute-start.13 = (bf16[512,128]{1,0:T(8,128)(2,1)S(1)}, bf16[512,128]{1,0:T(8,128)(2,1)S(1)}, u32[]{:S(2)}, u32[]{:S(2)}) collective-permute-start(bf16[512,128]{1,0:T(8,128)(2,1)S(1)} %get-tuple-element.67), channel_id=1, source_target_pairs={{0,4},{4,0},{8,12},{12,8},{16,20},{20,16},{24,28},{28,24},{32,36},... | collective-permute-start | bytes 393224 | tf_op jit(solution)/shard_map/ppermute | solution.py:302
  67.2 0.0 collective-permute-done.8.other
  67.2 2.3 %shard_map.83 = (bf16[128,8192]{1,0:T(8,128)(2,1)}, f32[8,128]{1,0:T(8,128)S(1)}) custom-call(s32[2]{0:T(128)S(1)} %pad_add_fusion.info, bf16[128,4096]{1,0:T(8,128)(2,1)S(1)} %get-tuple-element.55.mine, bf16[128,4096]{1,0:T(8,128)(2,1)S(1)} %collective-permute-done.8.other, bf16[512,128]{1,0:T(8,128)(2,1)S(1)} %get-tuple-element.60.after.refs_1_), custom_call_target="tpu_custom_call" | custom-call | tf_op jit(solution)/shard_map/pallas_call | solution.py:366
  69.5 0.0 collective-permute-done.12.refs_2_
  69.5 0.0 collective-permute-done.13.refs_3_
  69.5 1.5 %shard_map.85 = (bf16[128,1024]{1,0:T(8,128)(2,1)}, bf16[128,1024]{1,0:T(8,128)(2,1)}) custom-call(s32[2]{0:T(128)S(1)} %pad_add_fusion.info, bf16[512,128]{1,0:T(8,128)(2,1)S(1)} %get-tuple-element.65.refs_0_, bf16[512,128]{1,0:T(8,128)(2,1)S(1)} %get-tuple-element.60.after.refs_1_, bf16[512,128]{1,0:T(8,128)(2,1)S(1)} %collective-permute-done.12.refs_2_, ...), custom_call_target="tpu_custom_call" | custom-call | tf_op jit(solution)/shard_map/pallas_call | solution.py:375
Async XLA Ops:
  0.7 1.0 %copy-start.2 = (bf16[128,1024]{1,0:T(8,128)(2,1)S(1)}, bf16[128,1024]{1,0:T(8,128)(2,1)}, u32[]{:S(2)}) copy-start(bf16[128,1024]{1,0:T(8,128)(2,1)} %key_in.1) | copy-start | bytes 786436
  1.7 0.9 %copy-start.3 = (bf16[128,1024]{1,0:T(8,128)(2,1)S(1)}, bf16[128,1024]{1,0:T(8,128)(2,1)}, u32[]{:S(2)}) copy-start(bf16[128,1024]{1,0:T(8,128)(2,1)} %value_in.1) | copy-start | bytes 786436
  2.6 0.7 copy-start.4
  4.0 1.9 %collective-permute-start = (bf16[1040,128]{1,0:T(8,128)(2,1)S(1)}, bf16[1040,128]{1,0:T(8,128)(2,1)S(1)}, u32[]{:S(2)}, u32[]{:S(2)}) collective-permute-start(bf16[1040,128]{1,0:T(8,128)(2,1)S(1)} %get-tuple-element.38), channel_id=1, source_target_pairs={{0,4},{4,0},{8,12},{12,8},{16,20},{20,16},{24,28},{28,24},{32,36},... | collective-permute-start | bytes 798728 | tf_op jit(solution)/shard_map/ppermute | solution.py:302
  6.0 4.4 %collective-permute-start.3 = (bf16[128,8192]{1,0:T(8,128)(2,1)}, bf16[128,8192]{1,0:T(8,128)(2,1)S(1)}, u32[]{:S(2)}, u32[]{:S(2)}) collective-permute-start(bf16[128,8192]{1,0:T(8,128)(2,1)} %query.1), channel_id=1, source_target_pairs={{0,4},{4,0},{8,12},{12,8},{16,20},{20,16},{24,28},{28,24},{32,36},... | collective-permute-start | bytes 6291464 | tf_op jit(solution)/shard_map/ppermute | solution.py:302
  6.3 7.0 %collective-permute-start.4 = (bf16[128,8192]{1,0:T(8,128)(2,1)}, bf16[128,8192]{1,0:T(8,128)(2,1)S(1)}, u32[]{:S(2)}, u32[]{:S(2)}) collective-permute-start(bf16[128,8192]{1,0:T(8,128)(2,1)} %grad.1), channel_id=1, source_target_pairs={{0,4},{4,0},{8,12},{12,8},{16,20},{20,16},{24,28},{28,24},{32,36},... | collective-permute-start | bytes 6291464 | tf_op jit(solution)/shard_map/ppermute | solution.py:302
  7.1 13.6 %collective-permute-start.2 = (bf16[1040,128]{1,0:T(8,128)(2,1)S(1)}, bf16[1040,128]{1,0:T(8,128)(2,1)S(1)}, u32[]{:S(2)}, u32[]{:S(2)}) collective-permute-start(bf16[1040,128]{1,0:T(8,128)(2,1)S(1)} %get-tuple-element.40.kvo.refs_0_), channel_id=1, source_target_pairs={{0,16},{4,20},{8,24},{12,28},{16,32},{20,36},{24,40},{28,44},{32,4... | collective-permute-start | bytes 798728 | tf_op jit(solution)/shard_map/ppermute | solution.py:302
  7.7 13.5 %collective-permute-start.1 = (bf16[1040,128]{1,0:T(8,128)(2,1)S(1)}, bf16[1040,128]{1,0:T(8,128)(2,1)S(1)}, u32[]{:S(2)}, u32[]{:S(2)}) collective-permute-start(bf16[1040,128]{1,0:T(8,128)(2,1)S(1)} %get-tuple-element.40.kvo.refs_0_), channel_id=1, source_target_pairs={{0,8},{4,12},{8,16},{12,20},{16,24},{20,28},{24,32},{28,36},{32,40... | collective-permute-start | bytes 798728 | tf_op jit(solution)/shard_map/ppermute | solution.py:302
  13.3 1.6 %copy-start = (bf16[128,8192]{1,0:T(8,128)(2,1)S(1)}, bf16[128,8192]{1,0:T(8,128)(2,1)}, u32[]{:S(2)}) copy-start(bf16[128,8192]{1,0:T(8,128)(2,1)} %query.1) | copy-start | bytes 6291460
  14.9 1.6 %copy-start.1 = (bf16[128,8192]{1,0:T(8,128)(2,1)S(1)}, bf16[128,8192]{1,0:T(8,128)(2,1)}, u32[]{:S(2)}) copy-start(bf16[128,8192]{1,0:T(8,128)(2,1)} %grad.1) | copy-start | bytes 6291460
  18.2 15.5 %collective-permute-start.6 = (bf16[1040,128]{1,0:T(8,128)(2,1)S(1)}, bf16[1040,128]{1,0:T(8,128)(2,1)S(1)}, u32[]{:S(2)}, u32[]{:S(2)}) collective-permute-start(bf16[1040,128]{1,0:T(8,128)(2,1)S(1)} %get-tuple-element.49.kvo.refs_4_), channel_id=1, source_target_pairs={{0,16},{4,20},{8,24},{12,28},{16,32},{20,36},{24,40},{28,44},{32,4... | collective-permute-start | bytes 798728 | tf_op jit(solution)/shard_map/ppermute | solution.py:302
  18.7 14.9 %collective-permute-start.5 = (bf16[1040,128]{1,0:T(8,128)(2,1)S(1)}, bf16[1040,128]{1,0:T(8,128)(2,1)S(1)}, u32[]{:S(2)}, u32[]{:S(2)}) collective-permute-start(bf16[1040,128]{1,0:T(8,128)(2,1)S(1)} %get-tuple-element.49.kvo.refs_4_), channel_id=1, source_target_pairs={{0,8},{4,12},{8,16},{12,20},{16,24},{20,28},{24,32},{28,36},{32,40... | collective-permute-start | bytes 798728 | tf_op jit(solution)/shard_map/ppermute | solution.py:302
  27.5 12.5 %collective-permute-start.7 = (bf16[1024,128]{1,0:T(8,128)(2,1)S(1)}, bf16[1024,128]{1,0:T(8,128)(2,1)S(1)}, u32[]{:S(2)}, u32[]{:S(2)}) collective-permute-start(bf16[1024,128]{1,0:T(8,128)(2,1)S(1)} %get-tuple-element.53), channel_id=1, source_target_pairs={{0,248},{4,252},{8,0},{12,4},{16,8},{20,12},{24,16},{28,20},{32,24... | collective-permute-start | bytes 786440 | tf_op jit(solution)/shard_map/ppermute | solution.py:302
  28.7 22.0 %collective-permute-start.11 = (bf16[1024,128]{1,0:T(8,128)(2,1)S(1)}, bf16[1024,128]{1,0:T(8,128)(2,1)S(1)}, u32[]{:S(2)}, u32[]{:S(2)}) collective-permute-start(bf16[1024,128]{1,0:T(8,128)(2,1)S(1)} %get-tuple-element.64), channel_id=1, source_target_pairs={{0,240},{4,244},{8,248},{12,252},{16,0},{20,4},{24,8},{28,12},{32,... | collective-permute-start | bytes 786440 | tf_op jit(solution)/shard_map/ppermute | solution.py:302
  40.0 19.3 %collective-permute-start.9 = (bf16[1024,128]{1,0:T(8,128)(2,1)S(1)}, bf16[1024,128]{1,0:T(8,128)(2,1)S(1)}, u32[]{:S(2)}, u32[]{:S(2)}) collective-permute-start(bf16[1024,128]{1,0:T(8,128)(2,1)S(1)} %get-tuple-element.58), channel_id=1, source_target_pairs={{0,248},{4,252},{8,0},{12,4},{16,8},{20,12},{24,16},{28,20},{32,24... | collective-permute-start | bytes 786440 | tf_op jit(solution)/shard_map/ppermute | solution.py:302
  40.6 23.6 %collective-permute-start.10 = (bf16[1024,128]{1,0:T(8,128)(2,1)S(1)}, bf16[1024,128]{1,0:T(8,128)(2,1)S(1)}, u32[]{:S(2)}, u32[]{:S(2)}) collective-permute-start(bf16[1024,128]{1,0:T(8,128)(2,1)S(1)} %get-tuple-element.59), channel_id=1, source_target_pairs={{0,240},{4,244},{8,248},{12,252},{16,0},{20,4},{24,8},{28,12},{32,... | collective-permute-start | bytes 786440 | tf_op jit(solution)/shard_map/ppermute | solution.py:302
  51.4 18.2 %collective-permute-start.12 = (bf16[512,128]{1,0:T(8,128)(2,1)S(1)}, bf16[512,128]{1,0:T(8,128)(2,1)S(1)}, u32[]{:S(2)}, u32[]{:S(2)}) collective-permute-start(bf16[512,128]{1,0:T(8,128)(2,1)S(1)} %get-tuple-element.66), channel_id=1, source_target_pairs={{0,4},{4,0},{8,12},{12,8},{16,20},{20,16},{24,28},{28,24},{32,36},... | collective-permute-start | bytes 393224 | tf_op jit(solution)/shard_map/ppermute | solution.py:302
  59.2 8.0 %collective-permute-start.8 = (bf16[128,4096]{1,0:T(8,128)(2,1)S(1)}, bf16[128,4096]{1,0:T(8,128)(2,1)S(1)}, u32[]{:S(2)}, u32[]{:S(2)}) collective-permute-start(bf16[128,4096]{1,0:T(8,128)(2,1)S(1)} %get-tuple-element.56), channel_id=1, source_target_pairs={{0,4},{4,0},{8,12},{12,8},{16,20},{20,16},{24,28},{28,24},{32,36},... | collective-permute-start | bytes 3145736 | tf_op jit(solution)/shard_map/ppermute | solution.py:302
  64.8 4.8 %collective-permute-start.13 = (bf16[512,128]{1,0:T(8,128)(2,1)S(1)}, bf16[512,128]{1,0:T(8,128)(2,1)S(1)}, u32[]{:S(2)}, u32[]{:S(2)}) collective-permute-start(bf16[512,128]{1,0:T(8,128)(2,1)S(1)} %get-tuple-element.67), channel_id=1, source_target_pairs={{0,4},{4,0},{8,12},{12,8},{16,20},{20,16},{24,28},{28,24},{32,36},... | collective-permute-start | bytes 393224 | tf_op jit(solution)/shard_map/ppermute | solution.py:302
where the time goes:
time: 70.9 us; the launch traced here: 71 us
  Pallas kernels  25.3 us (36%)
  starting transfers between devices  24.8 us (35%)
  waiting for transfers between devices  14.4 us (20%)
  local copies, waits for them, and re-layouts  5.74 us (8%)
  between operations  0.75 us (1%)
    ppermute x14, starting transfers between devices, send(): return lax.ppermute(x, 'sp', perm)  24.8 us
    ppermute x14, waiting for transfers between devices, send(): return lax.ppermute(x, 'sp', perm)  14.4 us
    pallas_call x2, Pallas kernels, main_call(): pl.pallas_call(functools.partial(main_kernel, chunk), in_specs=[SMEM] + [...  12.7 us
    unnamed x10, local copies, waits for them, and re-layouts  5.74 us
    pallas_call x1, Pallas kernels, body(): pl.pallas_call(query_kernel, out_shape=(half, half), in_specs=[SMEM] + [V...  4.57 us
    pallas_call x1, Pallas kernels, body(): pl.pallas_call(place_kernel, out_shape=(shape(T, 2 * CORE_HEADS * GROUP *...  2.31 us
    pallas_call x1, Pallas kernels, body(): simple(stage_kernel, (stacked, stacked), 4)  1.62 us
    pallas_call x1, Pallas kernels, body(): pl.pallas_call(last_kernel, out_shape=(out, out), in_specs=[SMEM] + [VMEM...  1.47 us
  transfers between devices with their start and end apart: 14, of which 6 were waited for; matrix products, arithmetic and copies ran while one was open for 0% of the time, Pallas kernels for 32%

commit v1 on v0

--- a/solution.py
+++ b/solution.py
@@ -16,6 +16,7 @@
 HC = CORE_HEADS // CHUNKS
 PAY = HC * 512 + 16
 SMALL = 16 * 1024 * 1024
+BIG = 60 * 1024 * 1024
 ROWS = 128
 HALF = 512
 SCALE = D ** -0.5
@@ -31,8 +32,8 @@
     return pl.ds(pl.multiple_of(start, step), size)
 
 
-def prep_kernel(info, key_in, value_in, ids_in, mine, theirs, key, value, ids, sems):
-    c = info[0]
+def prep_kernel(key_in, value_in, ids_in, mine, theirs, key, value, ids, sems):
+    c = lax.axis_index("sp") % 2
     pairs = ((key_in, key), (value_in, value), (ids_in, ids))
     copies = [pltpu.make_async_copy(a, b, sems.at[i]) for i, (a, b) in enumerate(pairs)]
     for copy in copies:
@@ -207,16 +208,13 @@
                 out[n, i * T:(i + 1) * T, :] = part[:, rows(start + i * D, D)]
 
 
-def place_kernel(info, mine, other, after, out, token):
-    c = info[0]
-    width = CORE_HEADS * GROUP * D
-    for part, core in ((mine, c), (other, 1 - c)):
-        for i in range(0, width, D):
-            out[:, rows(core * width + i, D)] = part[:, i:i + D]
+def place_kernel(info, part, *refs):
+    out, token = refs[-2:]
+    out[...] = part[...]
     token[...] = jnp.zeros_like(token)
 
 
-def sum_kernel(info, own, b1, b2, mine, theirs):
+def sum_kernel(info, own, b1, b2, after, mine, theirs):
     c = info[0]
     for out, core in ((mine, c), (theirs, 1 - c)):
         for ht in range(2 * HC):
@@ -292,7 +290,7 @@
     devices = lax.axis_size("sp")
     me = lax.axis_index("sp")
     c, k = me % 2, me // 2
-    info = jnp.stack([c, k]).astype(jnp.int32)
+    info = jnp.stack([c, k, 1 - c]).astype(jnp.int32)
     swap = [(i, i ^ 1) for i in range(devices)]
 
     def ring(by):
@@ -305,14 +303,14 @@
     kv_in = pltpu.VMEM((T, 2 * CORE_HEADS * D), BF16)
     mine, theirs = pl.pallas_call(
         prep_kernel,
-        out_shape=(side, side),
-        in_specs=[SMEM, HBM, HBM, HBM],
+        out_shape=(pltpu.VMEM(side.shape, BF16),) * 2,
+        in_specs=[HBM, HBM, HBM],
         out_specs=(VMEM, VMEM),
         scratch_shapes=[
             kv_in, kv_in, pltpu.VMEM((1, T), jnp.int32), pltpu.SemaphoreType.DMA((3,))],
-        compiler_params=pltpu.CompilerParams(vmem_limit_bytes=SMALL),
+        compiler_params=pltpu.CompilerParams(vmem_limit_bytes=BIG),
         cost_estimate=FREE,
-    )(info, key_heads, value_heads, segment_ids.reshape(1, T))
+    )(key_heads, value_heads, segment_ids.reshape(1, T))
     other = send(theirs, swap)
     q_late, g_late, other = lax.optimization_barrier((queries, out_grad, other))
     q_other, g_other = send(q_late, swap), send(g_late, swap)
@@ -351,26 +349,38 @@
         cost_estimate=LONG,
     )(info, *score_grads)
     dq_other = send(dq_send, swap)
+    def place(core, part, after, *partial):
+        return pl.pallas_call(
+            place_kernel,
+            grid_spec=pltpu.PrefetchScalarGridSpec(
+                num_scalar_prefetch=1,
+                grid=(1,),
+                in_specs=[VMEM] + [ANY] * (1 + len(partial)),
+                out_specs=[
+                    pl.BlockSpec((T, CORE_HEADS * GROUP * D), lambda i, info: (0, info[core])),
+                    pl.BlockSpec((8, T), lambda i, info: (0, 0)),
+                ],
+            ),
+            out_shape=(shape(T, 2 * CORE_HEADS * GROUP * D), shape(8, T, dtype=F32)),
+            input_output_aliases={3: 0} if partial else {},
+            compiler_params=pltpu.CompilerParams(vmem_limit_bytes=SMALL),
+            cost_estimate=FREE,
+        )(info, part, after, *partial)
+
+    d_query, token = place(0, dq_mine, info)
     half = shape(2 * HC * T, T)
     for j in range(CHUNKS):
         a, b = pl.pallas_call(
             sum_kernel,
             out_shape=(half, half),
-            in_specs=[SMEM, VMEM, VMEM, VMEM],
+            in_specs=[SMEM, VMEM, VMEM, VMEM, ANY],
             out_specs=(VMEM, VMEM),
             compiler_params=pltpu.CompilerParams(vmem_limit_bytes=SMALL),
             cost_estimate=MID if j == CHUNKS - 1 else FREE,
-        )(info, *sums[j])
+        )(info, *sums[j], token if j == CHUNKS - 1 else info)
         kv_mine.append(a)
         kv_other.append(send(b, swap))
-    d_query, token = pl.pallas_call(
-        place_kernel,
-        out_shape=(shape(T, 2 * CORE_HEADS * GROUP * D), shape(8, T, dtype=F32)),
-        in_specs=[SMEM, VMEM, VMEM, ANY],
-        out_specs=(VMEM, VMEM),
-        compiler_params=pltpu.CompilerParams(vmem_limit_bytes=SMALL),
-        cost_estimate=FREE,
-    )(info, dq_mine, dq_other, kv_mine[-1])
+    d_query, token = place(2, dq_other, kv_mine[-1], d_query)
     out = shape(T, 2 * CORE_HEADS * D)
     d_key, d_value = pl.pallas_call(
         last_kernel,

time: 70.9 us -> 67.5 us (0.952)
  the two profiles are of different devices: /device:TPU:151 before, /device:TPU:51 now
where the time goes in v1:
time: 67.5 us; the launch traced here: 66.6 us
  Pallas kernels  30.7 us (45%)
  starting transfers between devices  18.7 us (28%)
  waiting for transfers between devices  13.2 us (20%)
  local copies, waits for them, and re-layouts  3.18 us (5%)
  between operations  0.73 us (1%)
    ppermute x14, starting transfers between devices, send(): return lax.ppermute(x, 'sp', perm)  18.7 us
    pallas_call x2, Pallas kernels, main_call(): pl.pallas_call(functools.partial(main_kernel, chunk), in_specs=[SMEM] + [...  15.1 us
    ppermute x14, waiting for transfers between devices, send(): return lax.ppermute(x, 'sp', perm)  13.2 us
    pallas_call x1, Pallas kernels, body(): pl.pallas_call(query_kernel, out_shape=(half, half), in_specs=[SMEM] + [V...  5.2 us
    unnamed x4, local copies, waits for them, and re-layouts  3.18 us
    pallas_call x2, Pallas kernels, place(): pl.pallas_call(place_kernel, grid_spec=pltpu.PrefetchScalarGridSpec(num_s...  3.15 us
    pallas_call x1, Pallas kernels, body(): simple(stage_kernel, (stacked, stacked), 4)  2.68 us
    pallas_call x1, Pallas kernels, body(): pl.pallas_call(last_kernel, out_shape=(out, out), in_specs=[SMEM] + [VMEM...  1.48 us
  transfers between devices with their start and end apart: 14, of which 6 were waited for; matrix products, arithmetic and copies ran while one was open for 0% of the time, Pallas kernels for 42%

profile of v1, /device:TPU:51, one launch (start us, length us, event | category | flops | bytes accessed | tf_op | source)
XLA Modules:
  0.0 66.6 jit_solution(5296987709901519492)
XLA Ops:
  0.6 1.2 %shard_map.76 = (bf16[1040,128]{1,0:T(8,128)(2,1)S(1)}, bf16[1040,128]{1,0:T(8,128)(2,1)S(1)}) custom-call(bf16[128,1024]{1,0:T(8,128)(2,1)} %key_in.1, bf16[128,1024]{1,0:T(8,128)(2,1)} %value_in.1, s32[1,128]{1,0:T(1,128)} %bitcast.4), custom_call_target="tpu_custom_call" | custom-call | tf_op jit(solution)/shard_map/pallas_call | solution.py:304
  1.8 0.8 %collective-permute-start = (bf16[1040,128]{1,0:T(8,128)(2,1)S(1)}, bf16[1040,128]{1,0:T(8,128)(2,1)S(1)}, u32[]{:S(2)}, u32[]{:S(2)}) collective-permute-start(bf16[1040,128]{1,0:T(8,128)(2,1)S(1)} %get-tuple-element.40), channel_id=1, source_target_pairs={{0,4},{4,0},{8,12},{12,8},{16,20},{20,16},{24,28},{28,24},{32,36},... | collective-permute-start | bytes 798728 | tf_op jit(solution)/shard_map/ppermute | solution.py:300
  2.6 1.2 %collective-permute-done.other = bf16[1040,128]{1,0:T(8,128)(2,1)S(1)} collective-permute-done((bf16[1040,128]{1,0:T(8,128)(2,1)S(1)}, bf16[1040,128]{1,0:T(8,128)(2,1)S(1)}, u32[]{:S(2)}, u32[]{:S(2)}) %collective-permute-start) | collective-permute-done | bytes 266272 | tf_op jit(solution)/shard_map/ppermute | solution.py:300
  3.8 0.4 collective-permute-start.3
  4.1 0.1 collective-permute-start.4
  4.3 0.1 pad_add_fusion.info.refs_0_.after
  4.3 0.6 shard_map.77
  4.9 1.5 %collective-permute-start.2 = (bf16[1040,128]{1,0:T(8,128)(2,1)S(1)}, bf16[1040,128]{1,0:T(8,128)(2,1)S(1)}, u32[]{:S(2)}, u32[]{:S(2)}) collective-permute-start(bf16[1040,128]{1,0:T(8,128)(2,1)S(1)} %get-tuple-element.42.kvo.refs_0_), channel_id=1, source_target_pairs={{0,16},{4,20},{8,24},{12,28},{16,32},{20,36},{24,40},{28,44},{32,4... | collective-permute-start | bytes 798728 | tf_op jit(solution)/shard_map/ppermute | solution.py:300
  6.4 1.9 %collective-permute-start.1 = (bf16[1040,128]{1,0:T(8,128)(2,1)S(1)}, bf16[1040,128]{1,0:T(8,128)(2,1)S(1)}, u32[]{:S(2)}, u32[]{:S(2)}) collective-permute-start(bf16[1040,128]{1,0:T(8,128)(2,1)S(1)} %get-tuple-element.42.kvo.refs_0_), channel_id=1, source_target_pairs={{0,8},{4,12},{8,16},{12,20},{16,24},{20,28},{24,32},{28,36},{32,40... | collective-permute-start | bytes 798728 | tf_op jit(solution)/shard_map/ppermute | solution.py:300
  8.3 1.4 %collective-permute-done.3.query_other = bf16[128,8192]{1,0:T(8,128)(2,1)S(1)} collective-permute-done((bf16[128,8192]{1,0:T(8,128)(2,1)}, bf16[128,8192]{1,0:T(8,128)(2,1)S(1)}, u32[]{:S(2)}, u32[]{:S(2)}) %collective-permute-start.3) | collective-permute-done | bytes 2097184 | tf_op jit(solution)/shard_map/ppermute | solution.py:300
  9.8 1.5 %collective-permute-done.4.grad_other = bf16[128,8192]{1,0:T(8,128)(2,1)} collective-permute-done((bf16[128,8192]{1,0:T(8,128)(2,1)}, bf16[128,8192]{1,0:T(8,128)(2,1)}, u32[]{:S(2)}, u32[]{:S(2)}) %collective-permute-start.4) | collective-permute-done | bytes 2097184 | tf_op jit(solution)/shard_map/ppermute | solution.py:300
  11.3 0.0 copy-start
  11.3 1.6 %copy-done = bf16[128,8192]{1,0:T(8,128)(2,1)S(1)} copy-done((bf16[128,8192]{1,0:T(8,128)(2,1)S(1)}, bf16[128,8192]{1,0:T(8,128)(2,1)}, u32[]{:S(2)}) %copy-start) | copy-done | bytes 2097176
  12.9 0.0 copy-start.1
  12.9 1.6 %copy-done.1 = bf16[128,8192]{1,0:T(8,128)(2,1)S(1)} copy-done((bf16[128,8192]{1,0:T(8,128)(2,1)S(1)}, bf16[128,8192]{1,0:T(8,128)(2,1)}, u32[]{:S(2)}) %copy-start.1) | copy-done | bytes 2097176
  14.4 2.7 %shard_map.78 = (bf16[2,4096,128]{2,1,0:T(8,128)(2,1)S(1)}, bf16[2,4096,128]{2,1,0:T(8,128)(2,1)S(1)}) custom-call(s32[3]{0:T(128)S(1)} %pad_add_fusion.info.refs_0_.after, bf16[128,8192]{1,0:T(8,128)(2,1)S(1)} %copy-done, bf16[128,8192]{1,0:T(8,128)(2,1)S(1)} %copy-done.1, bf16[128,8192]{1,0:T(8,128)(2,1)S(1)} %collective-permute-done.3.query_other, ...), custom_call_target="tpu_custom_call" | custom-call | tf_op jit(solution)/shard_map/pallas_call | solution.py:320
  17.1 1.5 %collective-permute-start.6 = (bf16[1040,128]{1,0:T(8,128)(2,1)S(1)}, bf16[1040,128]{1,0:T(8,128)(2,1)S(1)}, u32[]{:S(2)}, u32[]{:S(2)}) collective-permute-start(bf16[1040,128]{1,0:T(8,128)(2,1)S(1)} %get-tuple-element.51.kvo.refs_4_), channel_id=1, source_target_pairs={{0,16},{4,20},{8,24},{12,28},{16,32},{20,36},{24,40},{28,44},{32,4... | collective-permute-start | bytes 798728 | tf_op jit(solution)/shard_map/ppermute | solution.py:300
  18.6 1.9 %collective-permute-start.5 = (bf16[1040,128]{1,0:T(8,128)(2,1)S(1)}, bf16[1040,128]{1,0:T(8,128)(2,1)S(1)}, u32[]{:S(2)}, u32[]{:S(2)}) collective-permute-start(bf16[1040,128]{1,0:T(8,128)(2,1)S(1)} %get-tuple-element.51.kvo.refs_4_), channel_id=1, source_target_pairs={{0,8},{4,12},{8,16},{12,20},{16,24},{20,28},{24,32},{28,36},{32,40... | collective-permute-start | bytes 798728 | tf_op jit(solution)/shard_map/ppermute | solution.py:300
  20.5 0.0 collective-permute-done.2.kv2.refs_2_
  20.5 0.0 collective-permute-done.1.kv1.refs_1_
  20.5 7.5 %shard_map.79 = (f32[1024,128]{1,0:T(8,128)S(1)}, bf16[1024,128]{1,0:T(8,128)(2,1)S(1)}, bf16[1024,128]{1,0:T(8,128)(2,1)S(1)}, bf16[2,2,640,1024]{3,2,1,0:T(8,128)(2,1)S(1)}) custom-call(s32[3]{0:T(128)S(1)} %pad_add_fusion.info.refs_0_.after, bf16[1040,128]{1,0:T(8,128)(2,1)S(1)} %get-tuple-element.42.kvo.refs_0_, ...), custom_call_target="tpu_custom_call" | custom-call | flops 99999997952 | bytes 100000000 | tf_op jit(solution)/shard_map/pallas_call | solution.py:262
  28.1 0.1 collective-permute-start.7
  28.2 2.0 %collective-permute-start.11 = (bf16[1024,128]{1,0:T(8,128)(2,1)S(1)}, bf16[1024,128]{1,0:T(8,128)(2,1)S(1)}, u32[]{:S(2)}, u32[]{:S(2)}) collective-permute-start(bf16[1024,128]{1,0:T(8,128)(2,1)S(1)} %get-tuple-element.68), channel_id=1, source_target_pairs={{0,240},{4,244},{8,248},{12,252},{16,0},{20,4},{24,8},{28,12},{32,... | collective-permute-start | bytes 786440 | tf_op jit(solution)/shard_map/ppermute | solution.py:300
  30.2 0.0 collective-permute-done.6.kv2.refs_6_
  30.2 2.3 %collective-permute-done.5.kv1.refs_5_ = bf16[1040,128]{1,0:T(8,128)(2,1)S(1)} collective-permute-done((bf16[1040,128]{1,0:T(8,128)(2,1)S(1)}, bf16[1040,128]{1,0:T(8,128)(2,1)S(1)}, u32[]{:S(2)}, u32[]{:S(2)}) %collective-permute-start.5) | collective-permute-done | bytes 266272 | tf_op jit(solution)/shard_map/ppermute | solution.py:300
  32.6 7.5 %shard_map.80 = (f32[1024,128]{1,0:T(8,128)S(1)}, bf16[1024,128]{1,0:T(8,128)(2,1)S(1)}, bf16[1024,128]{1,0:T(8,128)(2,1)S(1)}, bf16[2,2,640,1024]{3,2,1,0:T(8,128)(2,1)S(1)}) custom-call(s32[3]{0:T(128)S(1)} %pad_add_fusion.info.refs_0_.after, bf16[1040,128]{1,0:T(8,128)(2,1)S(1)} %get-tuple-element.51.kvo.refs_4_, ...), custom_call_target="tpu_custom_call" | custom-call | flops 99999997952 | bytes 100000000 | tf_op jit(solution)/shard_map/pallas_call | solution.py:262
  40.1 0.0 collective-permute-done.7.b1
  40.1 0.1 collective-permute-start.9
  40.2 2.2 %collective-permute-start.10 = (bf16[1024,128]{1,0:T(8,128)(2,1)S(1)}, bf16[1024,128]{1,0:T(8,128)(2,1)S(1)}, u32[]{:S(2)}, u32[]{:S(2)}) collective-permute-start(bf16[1024,128]{1,0:T(8,128)(2,1)S(1)} %get-tuple-element.60), channel_id=1, source_target_pairs={{0,240},{4,244},{8,248},{12,252},{16,0},{20,4},{24,8},{28,12},{32,... | collective-permute-start | bytes 786440 | tf_op jit(solution)/shard_map/ppermute | solution.py:300
  42.4 4.8 %collective-permute-done.11.b2 = bf16[1024,128]{1,0:T(8,128)(2,1)S(1)} collective-permute-done((bf16[1024,128]{1,0:T(8,128)(2,1)S(1)}, bf16[1024,128]{1,0:T(8,128)(2,1)S(1)}, u32[]{:S(2)}, u32[]{:S(2)}) %collective-permute-start.11) | collective-permute-done | bytes 262176 | tf_op jit(solution)/shard_map/ppermute | solution.py:300
  47.1 0.6 shard_map.85
  47.8 3.6 %collective-permute-start.12 = (bf16[512,128]{1,0:T(8,128)(2,1)S(1)}, bf16[512,128]{1,0:T(8,128)(2,1)S(1)}, u32[]{:S(2)}, u32[]{:S(2)}) collective-permute-start(bf16[512,128]{1,0:T(8,128)(2,1)S(1)} %get-tuple-element.70), channel_id=1, source_target_pairs={{0,4},{4,0},{8,12},{12,8},{16,20},{20,16},{24,28},{28,24},{32,36},... | collective-permute-start | bytes 393224 | tf_op jit(solution)/shard_map/ppermute | solution.py:300
  51.4 5.2 %shard_map.81 = (bf16[128,4096]{1,0:T(8,128)(2,1)S(1)}, bf16[128,4096]{1,0:T(8,128)(2,1)S(1)}) custom-call(s32[3]{0:T(128)S(1)} %pad_add_fusion.info.refs_0_.after, bf16[1040,128]{1,0:T(8,128)(2,1)S(1)} %get-tuple-element.42.kvo.refs_0_, bf16[1040,128]{1,0:T(8,128)(2,1)S(1)} %collective-permute-done.1.kv1.refs_1_, ...), custom_call_target="tpu_custom_call" | custom-call | flops 99999997952 | bytes 100000000 | tf_op jit(solution)/shard_map/pallas_call | solution.py:337
  56.6 0.1 collective-permute-start.8
  56.7 1.6 %shard_map.82 = (bf16[128,8192]{1,0:T(8,128)(2,1)}, f32[8,128]{1,0:T(8,128)S(1)}) custom-call(s32[3]{0:T(128)S(1)} %pad_add_fusion.info.refs_0_.after, bf16[128,4096]{1,0:T(8,128)(2,1)S(1)} %get-tuple-element.61.part, s32[3]{0:T(128)S(1)} %pad_add_fusion.info.refs_0_.after), custom_call_target="tpu_custom_call" | custom-call | tf_op jit(solution)/shard_map/pallas_call | solution.py:353
  58.3 0.0 collective-permute-done.9.b1
  58.3 1.9 %collective-permute-done.10.b2 = bf16[1024,128]{1,0:T(8,128)(2,1)S(1)} collective-permute-done((bf16[1024,128]{1,0:T(8,128)(2,1)S(1)}, bf16[1024,128]{1,0:T(8,128)(2,1)S(1)}, u32[]{:S(2)}, u32[]{:S(2)}) %collective-permute-start.10) | collective-permute-done | bytes 262176 | tf_op jit(solution)/shard_map/ppermute | solution.py:300
  60.3 0.7 shard_map.83
  60.9 2.6 %collective-permute-start.13 = (bf16[512,128]{1,0:T(8,128)(2,1)S(1)}, bf16[512,128]{1,0:T(8,128)(2,1)S(1)}, u32[]{:S(2)}, u32[]{:S(2)}) collective-permute-start(bf16[512,128]{1,0:T(8,128)(2,1)S(1)} %get-tuple-element.71), channel_id=1, source_target_pairs={{0,4},{4,0},{8,12},{12,8},{16,20},{20,16},{24,28},{28,24},{32,36},... | collective-permute-start | bytes 393224 | tf_op jit(solution)/shard_map/ppermute | solution.py:300
  63.5 0.0 collective-permute-done.8.part
  63.5 1.6 %shard_map.84 = (bf16[128,8192]{1,0:T(8,128)(2,1)}, f32[8,128]{1,0:T(8,128)S(1)}) custom-call(s32[3]{0:T(128)S(1)} %pad_add_fusion.info.refs_0_.after, bf16[128,4096]{1,0:T(8,128)(2,1)S(1)} %collective-permute-done.8.part, bf16[512,128]{1,0:T(8,128)(2,1)S(1)} %get-tuple-element.63.refs_0_.refs_1_, ...), custom_call_target="tpu_custom_call", output_to_operand_aliasing={{0}: (3, {})} | custom-call | tf_op jit(solution)/shard_map/pallas_call | solution.py:353
  65.1 0.0 collective-permute-done.12.refs_2_
  65.1 0.0 collective-permute-done.13.refs_3_
  65.1 1.5 %shard_map.86 = (bf16[128,1024]{1,0:T(8,128)(2,1)}, bf16[128,1024]{1,0:T(8,128)(2,1)}) custom-call(s32[3]{0:T(128)S(1)} %pad_add_fusion.info.refs_0_.after, bf16[512,128]{1,0:T(8,128)(2,1)S(1)} %get-tuple-element.69.refs_0_, bf16[512,128]{1,0:T(8,128)(2,1)S(1)} %get-tuple-element.63.refs_0_.refs_1_, bf16[512,128]{1,0:T(8,128)(2,1)S(1)} %collective-permute-done.12.refs_2_, ...), custom_call_target="tpu_custom_call" | custom-call | tf_op jit(solution)/shard_map/pallas_call | solution.py:385
Async XLA Ops:
  1.8 1.9 %collective-permute-start = (bf16[1040,128]{1,0:T(8,128)(2,1)S(1)}, bf16[1040,128]{1,0:T(8,128)(2,1)S(1)}, u32[]{:S(2)}, u32[]{:S(2)}) collective-permute-start(bf16[1040,128]{1,0:T(8,128)(2,1)S(1)} %get-tuple-element.40), channel_id=1, source_target_pairs={{0,4},{4,0},{8,12},{12,8},{16,20},{20,16},{24,28},{28,24},{32,36},... | collective-permute-start | bytes 798728 | tf_op jit(solution)/shard_map/ppermute | solution.py:300
  3.8 6.0 %collective-permute-start.3 = (bf16[128,8192]{1,0:T(8,128)(2,1)}, bf16[128,8192]{1,0:T(8,128)(2,1)S(1)}, u32[]{:S(2)}, u32[]{:S(2)}) collective-permute-start(bf16[128,8192]{1,0:T(8,128)(2,1)} %query.1), channel_id=1, source_target_pairs={{0,4},{4,0},{8,12},{12,8},{16,20},{20,16},{24,28},{28,24},{32,36},... | collective-permute-start | bytes 6291464 | tf_op jit(solution)/shard_map/ppermute | solution.py:300
  4.1 7.1 %collective-permute-start.4 = (bf16[128,8192]{1,0:T(8,128)(2,1)}, bf16[128,8192]{1,0:T(8,128)(2,1)}, u32[]{:S(2)}, u32[]{:S(2)}) collective-permute-start(bf16[128,8192]{1,0:T(8,128)(2,1)} %grad.1), channel_id=1, source_target_pairs={{0,4},{4,0},{8,12},{12,8},{16,20},{20,16},{24,28},{28,24},{32,36},... | collective-permute-start | bytes 6291464 | tf_op jit(solution)/shard_map/ppermute | solution.py:300
  4.9 15.6 %collective-permute-start.2 = (bf16[1040,128]{1,0:T(8,128)(2,1)S(1)}, bf16[1040,128]{1,0:T(8,128)(2,1)S(1)}, u32[]{:S(2)}, u32[]{:S(2)}) collective-permute-start(bf16[1040,128]{1,0:T(8,128)(2,1)S(1)} %get-tuple-element.42.kvo.refs_0_), channel_id=1, source_target_pairs={{0,16},{4,20},{8,24},{12,28},{16,32},{20,36},{24,40},{28,44},{32,4... | collective-permute-start | bytes 798728 | tf_op jit(solution)/shard_map/ppermute | solution.py:300
  6.4 14.1 %collective-permute-start.1 = (bf16[1040,128]{1,0:T(8,128)(2,1)S(1)}, bf16[1040,128]{1,0:T(8,128)(2,1)S(1)}, u32[]{:S(2)}, u32[]{:S(2)}) collective-permute-start(bf16[1040,128]{1,0:T(8,128)(2,1)S(1)} %get-tuple-element.42.kvo.refs_0_), channel_id=1, source_target_pairs={{0,8},{4,12},{8,16},{12,20},{16,24},{20,28},{24,32},{28,36},{32,40... | collective-permute-start | bytes 798728 | tf_op jit(solution)/shard_map/ppermute | solution.py:300
  11.3 1.6 %copy-start = (bf16[128,8192]{1,0:T(8,128)(2,1)S(1)}, bf16[128,8192]{1,0:T(8,128)(2,1)}, u32[]{:S(2)}) copy-start(bf16[128,8192]{1,0:T(8,128)(2,1)} %query.1) | copy-start | bytes 6291460
  12.9 1.6 %copy-start.1 = (bf16[128,8192]{1,0:T(8,128)(2,1)S(1)}, bf16[128,8192]{1,0:T(8,128)(2,1)}, u32[]{:S(2)}) copy-start(bf16[128,8192]{1,0:T(8,128)(2,1)} %grad.1) | copy-start | bytes 6291460
  17.1 13.1 %collective-permute-start.6 = (bf16[1040,128]{1,0:T(8,128)(2,1)S(1)}, bf16[1040,128]{1,0:T(8,128)(2,1)S(1)}, u32[]{:S(2)}, u32[]{:S(2)}) collective-permute-start(bf16[1040,128]{1,0:T(8,128)(2,1)S(1)} %get-tuple-element.51.kvo.refs_4_), channel_id=1, source_target_pairs={{0,16},{4,20},{8,24},{12,28},{16,32},{20,36},{24,40},{28,44},{32,4... | collective-permute-start | bytes 798728 | tf_op jit(solution)/shard_map/ppermute | solution.py:300
  18.6 13.9 %collective-permute-start.5 = (bf16[1040,128]{1,0:T(8,128)(2,1)S(1)}, bf16[1040,128]{1,0:T(8,128)(2,1)S(1)}, u32[]{:S(2)}, u32[]{:S(2)}) collective-permute-start(bf16[1040,128]{1,0:T(8,128)(2,1)S(1)} %get-tuple-element.51.kvo.refs_4_), channel_id=1, source_target_pairs={{0,8},{4,12},{8,16},{12,20},{16,24},{20,28},{24,32},{28,36},{32,40... | collective-permute-start | bytes 798728 | tf_op jit(solution)/shard_map/ppermute | solution.py:300
  28.1 12.0 %collective-permute-start.7 = (bf16[1024,128]{1,0:T(8,128)(2,1)S(1)}, bf16[1024,128]{1,0:T(8,128)(2,1)S(1)}, u32[]{:S(2)}, u32[]{:S(2)}) collective-permute-start(bf16[1024,128]{1,0:T(8,128)(2,1)S(1)} %get-tuple-element.55), channel_id=1, source_target_pairs={{0,248},{4,252},{8,0},{12,4},{16,8},{20,12},{24,16},{28,20},{32,24... | collective-permute-start | bytes 786440 | tf_op jit(solution)/shard_map/ppermute | solution.py:300
  28.2 19.0 %collective-permute-start.11 = (bf16[1024,128]{1,0:T(8,128)(2,1)S(1)}, bf16[1024,128]{1,0:T(8,128)(2,1)S(1)}, u32[]{:S(2)}, u32[]{:S(2)}) collective-permute-start(bf16[1024,128]{1,0:T(8,128)(2,1)S(1)} %get-tuple-element.68), channel_id=1, source_target_pairs={{0,240},{4,244},{8,248},{12,252},{16,0},{20,4},{24,8},{28,12},{32,... | collective-permute-start | bytes 786440 | tf_op jit(solution)/shard_map/ppermute | solution.py:300
  40.1 18.2 %collective-permute-start.9 = (bf16[1024,128]{1,0:T(8,128)(2,1)S(1)}, bf16[1024,128]{1,0:T(8,128)(2,1)S(1)}, u32[]{:S(2)}, u32[]{:S(2)}) collective-permute-start(bf16[1024,128]{1,0:T(8,128)(2,1)S(1)} %get-tuple-element.59), channel_id=1, source_target_pairs={{0,248},{4,252},{8,0},{12,4},{16,8},{20,12},{24,16},{28,20},{32,24... | collective-permute-start | bytes 786440 | tf_op jit(solution)/shard_map/ppermute | solution.py:300
  40.2 20.0 %collective-permute-start.10 = (bf16[1024,128]{1,0:T(8,128)(2,1)S(1)}, bf16[1024,128]{1,0:T(8,128)(2,1)S(1)}, u32[]{:S(2)}, u32[]{:S(2)}) collective-permute-start(bf16[1024,128]{1,0:T(8,128)(2,1)S(1)} %get-tuple-element.60), channel_id=1, source_target_pairs={{0,240},{4,244},{8,248},{12,252},{16,0},{20,4},{24,8},{28,12},{32,... | collective-permute-start | bytes 786440 | tf_op jit(solution)/shard_map/ppermute | solution.py:300
  47.8 17.3 %collective-permute-start.12 = (bf16[512,128]{1,0:T(8,128)(2,1)S(1)}, bf16[512,128]{1,0:T(8,128)(2,1)S(1)}, u32[]{:S(2)}, u32[]{:S(2)}) collective-permute-start(bf16[512,128]{1,0:T(8,128)(2,1)S(1)} %get-tuple-element.70), channel_id=1, source_target_pairs={{0,4},{4,0},{8,12},{12,8},{16,20},{20,16},{24,28},{28,24},{32,36},... | collective-permute-start | bytes 393224 | tf_op jit(solution)/shard_map/ppermute | solution.py:300
  56.6 6.9 %collective-permute-start.8 = (bf16[128,4096]{1,0:T(8,128)(2,1)S(1)}, bf16[128,4096]{1,0:T(8,128)(2,1)S(1)}, u32[]{:S(2)}, u32[]{:S(2)}) collective-permute-start(bf16[128,4096]{1,0:T(8,128)(2,1)S(1)} %get-tuple-element.57), channel_id=1, source_target_pairs={{0,4},{4,0},{8,12},{12,8},{16,20},{20,16},{24,28},{28,24},{32,36},... | collective-permute-start | bytes 3145736 | tf_op jit(solution)/shard_map/ppermute | solution.py:300
  60.9 4.2 %collective-permute-start.13 = (bf16[512,128]{1,0:T(8,128)(2,1)S(1)}, bf16[512,128]{1,0:T(8,128)(2,1)S(1)}, u32[]{:S(2)}, u32[]{:S(2)}) collective-permute-start(bf16[512,128]{1,0:T(8,128)(2,1)S(1)} %get-tuple-element.71), channel_id=1, source_target_pairs={{0,4},{4,0},{8,12},{12,8},{16,20},{20,16},{24,28},{28,24},{32,36},... | collective-permute-start | bytes 393224 | tf_op jit(solution)/shard_map/ppermute | solution.py:300

commit v2 on v1

--- a/solution.py
+++ b/solution.py
@@ -17,7 +17,7 @@
 PAY = HC * 512 + 16
 SMALL = 16 * 1024 * 1024
 BIG = 60 * 1024 * 1024
-ROWS = 128
+ROWS = 64
 HALF = 512
 SCALE = D ** -0.5
 LOG2E = 1.4426950408889634
@@ -325,10 +325,6 @@
     sums, score_grads, kv_mine, kv_other = [], [], [], []
     for j in range(CHUNKS):
         own, out1, out2, ds = main_call(j, info, payloads[j], *came[j], qs, gs)
-        if sums:
-            own_a, near_a, far_a = sums[-1]
-            out1, out2, ds, near_a = lax.optimization_barrier((out1, out2, ds, near_a))
-            sums[-1] = own_a, near_a, far_a
         b2 = send(out2, ring(-4))
         b1 = send(out1, ring(-2))
         sums.append((own, b1, b2))
@@ -377,7 +373,7 @@
             out_specs=(VMEM, VMEM),
             compiler_params=pltpu.CompilerParams(vmem_limit_bytes=SMALL),
             cost_estimate=MID if j == CHUNKS - 1 else FREE,
-        )(info, *sums[j], token if j == CHUNKS - 1 else info)
+        )(info, *sums[j], token if j == CHUNKS - 1 else sums[-1][0])
         kv_mine.append(a)
         kv_other.append(send(b, swap))
     d_query, token = place(2, dq_other, kv_mine[-1], d_query)

time: 67.5 us -> 68.2 us (1.010)
  the two profiles are of different devices: /device:TPU:51 before, /device:TPU:19 now
where the time goes in v2:
time: 68.2 us; the launch traced here: 68 us
  Pallas kernels  27.7 us (41%)
  starting transfers between devices  27.3 us (40%)
  waiting for transfers between devices  9.06 us (13%)
  local copies, waits for them, and re-layouts  3.18 us (5%)
  between operations  0.72 us (1%)
    ppermute x14, starting transfers between devices, send(): return lax.ppermute(x, 'sp', perm)  27.3 us
    pallas_call x2, Pallas kernels, main_call(): pl.pallas_call(functools.partial(main_kernel, chunk), in_specs=[SMEM] + [...  12.8 us
    ppermute x14, waiting for transfers between devices, send(): return lax.ppermute(x, 'sp', perm)  9.06 us
    pallas_call x1, Pallas kernels, body(): pl.pallas_call(query_kernel, out_shape=(half, half), in_specs=[SMEM] + [V...  4.56 us
    unnamed x4, local copies, waits for them, and re-layouts  3.18 us
    pallas_call x2, Pallas kernels, place(): pl.pallas_call(place_kernel, grid_spec=pltpu.PrefetchScalarGridSpec(num_s...  3.16 us
    pallas_call x1, Pallas kernels, body(): simple(stage_kernel, (stacked, stacked), 4)  2.68 us
    pallas_call x1, Pallas kernels, body(): pl.pallas_call(last_kernel, out_shape=(out, out), in_specs=[SMEM] + [VMEM...  1.48 us
  transfers between devices with their start and end apart: 14, of which 5 were waited for; matrix products, arithmetic and copies ran while one was open for 0% of the time, Pallas kernels for 37%

profile of v2, /device:TPU:19, one launch (start us, length us, event | category | flops | bytes accessed | tf_op | source)
XLA Modules:
  0.0 68.0 jit_solution(2473412209593269411)
XLA Ops:
  0.6 1.2 %shard_map.76 = (bf16[1040,128]{1,0:T(8,128)(2,1)S(1)}, bf16[1040,128]{1,0:T(8,128)(2,1)S(1)}) custom-call(bf16[128,1024]{1,0:T(8,128)(2,1)} %key_in.1, bf16[128,1024]{1,0:T(8,128)(2,1)} %value_in.1, s32[1,128]{1,0:T(1,128)} %bitcast.4), custom_call_target="tpu_custom_call" | custom-call | tf_op jit(solution)/shard_map/pallas_call | solution.py:304
  1.8 0.8 %collective-permute-start = (bf16[1040,128]{1,0:T(8,128)(2,1)S(1)}, bf16[1040,128]{1,0:T(8,128)(2,1)S(1)}, u32[]{:S(2)}, u32[]{:S(2)}) collective-permute-start(bf16[1040,128]{1,0:T(8,128)(2,1)S(1)} %get-tuple-element.36), channel_id=1, source_target_pairs={{0,4},{4,0},{8,12},{12,8},{16,20},{20,16},{24,28},{28,24},{32,36},... | collective-permute-start | bytes 798728 | tf_op jit(solution)/shard_map/ppermute | solution.py:300
  2.6 1.2 %collective-permute-done.other = bf16[1040,128]{1,0:T(8,128)(2,1)S(1)} collective-permute-done((bf16[1040,128]{1,0:T(8,128)(2,1)S(1)}, bf16[1040,128]{1,0:T(8,128)(2,1)S(1)}, u32[]{:S(2)}, u32[]{:S(2)}) %collective-permute-start) | collective-permute-done | bytes 266272 | tf_op jit(solution)/shard_map/ppermute | solution.py:300
  3.8 0.4 collective-permute-start.3
  4.1 0.1 collective-permute-start.4
  4.3 0.1 pad_add_fusion.info.refs_0_
  4.3 0.6 shard_map.77
  4.9 1.5 %collective-permute-start.2 = (bf16[1040,128]{1,0:T(8,128)(2,1)S(1)}, bf16[1040,128]{1,0:T(8,128)(2,1)S(1)}, u32[]{:S(2)}, u32[]{:S(2)}) collective-permute-start(bf16[1040,128]{1,0:T(8,128)(2,1)S(1)} %get-tuple-element.38.kvo.refs_0_), channel_id=1, source_target_pairs={{0,16},{4,20},{8,24},{12,28},{16,32},{20,36},{24,40},{28,44},{32,4... | collective-permute-start | bytes 798728 | tf_op jit(solution)/shard_map/ppermute | solution.py:300
  6.4 1.9 %collective-permute-start.1 = (bf16[1040,128]{1,0:T(8,128)(2,1)S(1)}, bf16[1040,128]{1,0:T(8,128)(2,1)S(1)}, u32[]{:S(2)}, u32[]{:S(2)}) collective-permute-start(bf16[1040,128]{1,0:T(8,128)(2,1)S(1)} %get-tuple-element.38.kvo.refs_0_), channel_id=1, source_target_pairs={{0,8},{4,12},{8,16},{12,20},{16,24},{20,28},{24,32},{28,36},{32,40... | collective-permute-start | bytes 798728 | tf_op jit(solution)/shard_map/ppermute | solution.py:300
  8.3 1.4 %collective-permute-done.3.query_other = bf16[128,8192]{1,0:T(8,128)(2,1)S(1)} collective-permute-done((bf16[128,8192]{1,0:T(8,128)(2,1)}, bf16[128,8192]{1,0:T(8,128)(2,1)S(1)}, u32[]{:S(2)}, u32[]{:S(2)}) %collective-permute-start.3) | collective-permute-done | bytes 2097184 | tf_op jit(solution)/shard_map/ppermute | solution.py:300
  9.8 1.5 %collective-permute-done.4.grad_other = bf16[128,8192]{1,0:T(8,128)(2,1)} collective-permute-done((bf16[128,8192]{1,0:T(8,128)(2,1)}, bf16[128,8192]{1,0:T(8,128)(2,1)}, u32[]{:S(2)}, u32[]{:S(2)}) %collective-permute-start.4) | collective-permute-done | bytes 2097184 | tf_op jit(solution)/shard_map/ppermute | solution.py:300
  11.3 0.0 copy-start
  11.3 1.6 %copy-done = bf16[128,8192]{1,0:T(8,128)(2,1)S(1)} copy-done((bf16[128,8192]{1,0:T(8,128)(2,1)S(1)}, bf16[128,8192]{1,0:T(8,128)(2,1)}, u32[]{:S(2)}) %copy-start) | copy-done | bytes 2097176
  12.9 0.0 copy-start.1
  12.9 1.6 %copy-done.1 = bf16[128,8192]{1,0:T(8,128)(2,1)S(1)} copy-done((bf16[128,8192]{1,0:T(8,128)(2,1)S(1)}, bf16[128,8192]{1,0:T(8,128)(2,1)}, u32[]{:S(2)}) %copy-start.1) | copy-done | bytes 2097176
  14.4 2.7 %shard_map.78 = (bf16[2,4096,128]{2,1,0:T(8,128)(2,1)S(1)}, bf16[2,4096,128]{2,1,0:T(8,128)(2,1)S(1)}) custom-call(s32[3]{0:T(128)S(1)} %pad_add_fusion.info.refs_0_, bf16[128,8192]{1,0:T(8,128)(2,1)S(1)} %copy-done, bf16[128,8192]{1,0:T(8,128)(2,1)S(1)} %copy-done.1, bf16[128,8192]{1,0:T(8,128)(2,1)S(1)} %collective-permute-done.3.query_other, ...), custom_call_target="tpu_custom_call" | custom-call | tf_op jit(solution)/shard_map/pallas_call | solution.py:320
  17.1 1.5 %collective-permute-start.6 = (bf16[1040,128]{1,0:T(8,128)(2,1)S(1)}, bf16[1040,128]{1,0:T(8,128)(2,1)S(1)}, u32[]{:S(2)}, u32[]{:S(2)}) collective-permute-start(bf16[1040,128]{1,0:T(8,128)(2,1)S(1)} %get-tuple-element.47.kvo.refs_4_), channel_id=1, source_target_pairs={{0,16},{4,20},{8,24},{12,28},{16,32},{20,36},{24,40},{28,44},{32,4... | collective-permute-start | bytes 798728 | tf_op jit(solution)/shard_map/ppermute | solution.py:300
  18.6 1.9 %collective-permute-start.5 = (bf16[1040,128]{1,0:T(8,128)(2,1)S(1)}, bf16[1040,128]{1,0:T(8,128)(2,1)S(1)}, u32[]{:S(2)}, u32[]{:S(2)}) collective-permute-start(bf16[1040,128]{1,0:T(8,128)(2,1)S(1)} %get-tuple-element.47.kvo.refs_4_), channel_id=1, source_target_pairs={{0,8},{4,12},{8,16},{12,20},{16,24},{20,28},{24,32},{28,36},{32,40... | collective-permute-start | bytes 798728 | tf_op jit(solution)/shard_map/ppermute | solution.py:300
  20.5 0.0 collective-permute-done.2.kv2.refs_2_
  20.5 0.0 collective-permute-done.1.kv1.refs_1_
  20.5 6.4 %shard_map.79 = (f32[1024,128]{1,0:T(8,128)S(1)}, bf16[1024,128]{1,0:T(8,128)(2,1)S(1)}, bf16[1024,128]{1,0:T(8,128)(2,1)S(1)}, bf16[2,2,640,1024]{3,2,1,0:T(8,128)(2,1)S(1)}) custom-call(s32[3]{0:T(128)S(1)} %pad_add_fusion.info.refs_0_, bf16[1040,128]{1,0:T(8,128)(2,1)S(1)} %get-tuple-element.38.kvo.refs_0_, ...), custom_call_target="tpu_custom_call" | custom-call | flops 99999997952 | bytes 100000000 | tf_op jit(solution)/shard_map/pallas_call | solution.py:262
  26.9 0.1 collective-permute-start.10
  27.0 7.7 %collective-permute-start.11 = (bf16[1024,128]{1,0:T(8,128)(2,1)S(1)}, bf16[1024,128]{1,0:T(8,128)(2,1)S(1)}, u32[]{:S(2)}, u32[]{:S(2)}) collective-permute-start(bf16[1024,128]{1,0:T(8,128)(2,1)S(1)} %get-tuple-element.60), channel_id=1, source_target_pairs={{0,240},{4,244},{8,248},{12,252},{16,0},{20,4},{24,8},{28,12},{32,... | collective-permute-start | bytes 786440 | tf_op jit(solution)/shard_map/ppermute | solution.py:300
  34.8 0.0 collective-permute-done.6.kv2.refs_6_
  34.8 0.0 collective-permute-done.5.kv1.refs_5_
  34.8 6.4 %shard_map.80 = (f32[1024,128]{1,0:T(8,128)S(1)}, bf16[1024,128]{1,0:T(8,128)(2,1)S(1)}, bf16[1024,128]{1,0:T(8,128)(2,1)S(1)}, bf16[2,2,640,1024]{3,2,1,0:T(8,128)(2,1)S(1)}) custom-call(s32[3]{0:T(128)S(1)} %pad_add_fusion.info.refs_0_, bf16[1040,128]{1,0:T(8,128)(2,1)S(1)} %get-tuple-element.47.kvo.refs_4_, ...), custom_call_target="tpu_custom_call" | custom-call | flops 99999997952 | bytes 100000000 | tf_op jit(solution)/shard_map/pallas_call | solution.py:262
  41.2 0.1 collective-permute-start.8
  41.3 5.7 %collective-permute-start.9 = (bf16[1024,128]{1,0:T(8,128)(2,1)S(1)}, bf16[1024,128]{1,0:T(8,128)(2,1)S(1)}, u32[]{:S(2)}, u32[]{:S(2)}) collective-permute-start(bf16[1024,128]{1,0:T(8,128)(2,1)S(1)} %get-tuple-element.52), channel_id=1, source_target_pairs={{0,240},{4,244},{8,248},{12,252},{16,0},{20,4},{24,8},{28,12},{32,... | collective-permute-start | bytes 786440 | tf_op jit(solution)/shard_map/ppermute | solution.py:300
  47.0 0.0 collective-permute-done.10.b1
  47.0 1.3 %collective-permute-done.11.b2 = bf16[1024,128]{1,0:T(8,128)(2,1)S(1)} collective-permute-done((bf16[1024,128]{1,0:T(8,128)(2,1)S(1)}, bf16[1024,128]{1,0:T(8,128)(2,1)S(1)}, u32[]{:S(2)}, u32[]{:S(2)}) %collective-permute-start.11) | collective-permute-done | bytes 262176 | tf_op jit(solution)/shard_map/ppermute | solution.py:300
  48.3 0.6 shard_map.85
  48.9 3.7 %collective-permute-start.12 = (bf16[512,128]{1,0:T(8,128)(2,1)S(1)}, bf16[512,128]{1,0:T(8,128)(2,1)S(1)}, u32[]{:S(2)}, u32[]{:S(2)}) collective-permute-start(bf16[512,128]{1,0:T(8,128)(2,1)S(1)} %get-tuple-element.62), channel_id=1, source_target_pairs={{0,4},{4,0},{8,12},{12,8},{16,20},{20,16},{24,28},{28,24},{32,36},... | collective-permute-start | bytes 393224 | tf_op jit(solution)/shard_map/ppermute | solution.py:300
  52.6 4.6 %shard_map.81 = (bf16[128,4096]{1,0:T(8,128)(2,1)S(1)}, bf16[128,4096]{1,0:T(8,128)(2,1)S(1)}) custom-call(s32[3]{0:T(128)S(1)} %pad_add_fusion.info.refs_0_, bf16[1040,128]{1,0:T(8,128)(2,1)S(1)} %get-tuple-element.38.kvo.refs_0_, bf16[1040,128]{1,0:T(8,128)(2,1)S(1)} %collective-permute-done.1.kv1.refs_1_, ...), custom_call_target="tpu_custom_call" | custom-call | flops 99999997952 | bytes 100000000 | tf_op jit(solution)/shard_map/pallas_call | solution.py:333
  57.1 1.6 %shard_map.82 = (bf16[128,8192]{1,0:T(8,128)(2,1)}, f32[8,128]{1,0:T(8,128)S(1)}) custom-call(s32[3]{0:T(128)S(1)} %pad_add_fusion.info.refs_0_, bf16[128,4096]{1,0:T(8,128)(2,1)S(1)} %get-tuple-element.53.part, s32[3]{0:T(128)S(1)} %pad_add_fusion.info.refs_0_), custom_call_target="tpu_custom_call" | custom-call | tf_op jit(solution)/shard_map/pallas_call | solution.py:349
  58.7 0.0 collective-permute-start.7
  58.7 0.0 collective-permute-done.8.b1
  58.7 3.6 %collective-permute-done.9.b2 = bf16[1024,128]{1,0:T(8,128)(2,1)S(1)} collective-permute-done((bf16[1024,128]{1,0:T(8,128)(2,1)S(1)}, bf16[1024,128]{1,0:T(8,128)(2,1)S(1)}, u32[]{:S(2)}, u32[]{:S(2)}) %collective-permute-start.9) | collective-permute-done | bytes 262176 | tf_op jit(solution)/shard_map/ppermute | solution.py:300
  62.4 0.6 shard_map.83
  63.0 1.9 %collective-permute-start.13 = (bf16[512,128]{1,0:T(8,128)(2,1)S(1)}, bf16[512,128]{1,0:T(8,128)(2,1)S(1)}, u32[]{:S(2)}, u32[]{:S(2)}) collective-permute-start(bf16[512,128]{1,0:T(8,128)(2,1)S(1)} %get-tuple-element.63), channel_id=1, source_target_pairs={{0,4},{4,0},{8,12},{12,8},{16,20},{20,16},{24,28},{28,24},{32,36},... | collective-permute-start | bytes 393224 | tf_op jit(solution)/shard_map/ppermute | solution.py:300
  65.0 0.0 collective-permute-done.7.part
  65.0 1.6 %shard_map.84 = (bf16[128,8192]{1,0:T(8,128)(2,1)}, f32[8,128]{1,0:T(8,128)S(1)}) custom-call(s32[3]{0:T(128)S(1)} %pad_add_fusion.info.refs_0_, bf16[128,4096]{1,0:T(8,128)(2,1)S(1)} %collective-permute-done.7.part, bf16[512,128]{1,0:T(8,128)(2,1)S(1)} %get-tuple-element.55.refs_0_.refs_1_, ...), custom_call_target="tpu_custom_call", output_to_operand_aliasing={{0}: (3, {})} | custom-call | tf_op jit(solution)/shard_map/pallas_call | solution.py:349
  66.5 0.0 collective-permute-done.12.refs_2_
  66.5 0.0 collective-permute-done.13.refs_3_
  66.5 1.5 %shard_map.86 = (bf16[128,1024]{1,0:T(8,128)(2,1)}, bf16[128,1024]{1,0:T(8,128)(2,1)}) custom-call(s32[3]{0:T(128)S(1)} %pad_add_fusion.info.refs_0_, bf16[512,128]{1,0:T(8,128)(2,1)S(1)} %get-tuple-element.61.refs_0_, bf16[512,128]{1,0:T(8,128)(2,1)S(1)} %get-tuple-element.55.refs_0_.refs_1_, bf16[512,128]{1,0:T(8,128)(2,1)S(1)} %collective-permute-done.12.refs_2_, ...), custom_call_target="tpu_custom_call" | custom-call | tf_op jit(solution)/shard_map/pallas_call | solution.py:381
Async XLA Ops:
  1.8 1.9 %collective-permute-start = (bf16[1040,128]{1,0:T(8,128)(2,1)S(1)}, bf16[1040,128]{1,0:T(8,128)(2,1)S(1)}, u32[]{:S(2)}, u32[]{:S(2)}) collective-permute-start(bf16[1040,128]{1,0:T(8,128)(2,1)S(1)} %get-tuple-element.36), channel_id=1, source_target_pairs={{0,4},{4,0},{8,12},{12,8},{16,20},{20,16},{24,28},{28,24},{32,36},... | collective-permute-start | bytes 798728 | tf_op jit(solution)/shard_map/ppermute | solution.py:300
  3.8 6.0 %collective-permute-start.3 = (bf16[128,8192]{1,0:T(8,128)(2,1)}, bf16[128,8192]{1,0:T(8,128)(2,1)S(1)}, u32[]{:S(2)}, u32[]{:S(2)}) collective-permute-start(bf16[128,8192]{1,0:T(8,128)(2,1)} %query.1), channel_id=1, source_target_pairs={{0,4},{4,0},{8,12},{12,8},{16,20},{20,16},{24,28},{28,24},{32,36},... | collective-permute-start | bytes 6291464 | tf_op jit(solution)/shard_map/ppermute | solution.py:300
  4.1 7.1 %collective-permute-start.4 = (bf16[128,8192]{1,0:T(8,128)(2,1)}, bf16[128,8192]{1,0:T(8,128)(2,1)}, u32[]{:S(2)}, u32[]{:S(2)}) collective-permute-start(bf16[128,8192]{1,0:T(8,128)(2,1)} %grad.1), channel_id=1, source_target_pairs={{0,4},{4,0},{8,12},{12,8},{16,20},{20,16},{24,28},{28,24},{32,36},... | collective-permute-start | bytes 6291464 | tf_op jit(solution)/shard_map/ppermute | solution.py:300
  4.9 15.6 %collective-permute-start.2 = (bf16[1040,128]{1,0:T(8,128)(2,1)S(1)}, bf16[1040,128]{1,0:T(8,128)(2,1)S(1)}, u32[]{:S(2)}, u32[]{:S(2)}) collective-permute-start(bf16[1040,128]{1,0:T(8,128)(2,1)S(1)} %get-tuple-element.38.kvo.refs_0_), channel_id=1, source_target_pairs={{0,16},{4,20},{8,24},{12,28},{16,32},{20,36},{24,40},{28,44},{32,4... | collective-permute-start | bytes 798728 | tf_op jit(solution)/shard_map/ppermute | solution.py:300
  6.4 14.1 %collective-permute-start.1 = (bf16[1040,128]{1,0:T(8,128)(2,1)S(1)}, bf16[1040,128]{1,0:T(8,128)(2,1)S(1)}, u32[]{:S(2)}, u32[]{:S(2)}) collective-permute-start(bf16[1040,128]{1,0:T(8,128)(2,1)S(1)} %get-tuple-element.38.kvo.refs_0_), channel_id=1, source_target_pairs={{0,8},{4,12},{8,16},{12,20},{16,24},{20,28},{24,32},{28,36},{32,40... | collective-permute-start | bytes 798728 | tf_op jit(solution)/shard_map/ppermute | solution.py:300
  11.3 1.6 %copy-start = (bf16[128,8192]{1,0:T(8,128)(2,1)S(1)}, bf16[128,8192]{1,0:T(8,128)(2,1)}, u32[]{:S(2)}) copy-start(bf16[128,8192]{1,0:T(8,128)(2,1)} %query.1) | copy-start | bytes 6291460
  12.9 1.6 %copy-start.1 = (bf16[128,8192]{1,0:T(8,128)(2,1)S(1)}, bf16[128,8192]{1,0:T(8,128)(2,1)}, u32[]{:S(2)}) copy-start(bf16[128,8192]{1,0:T(8,128)(2,1)} %grad.1) | copy-start | bytes 6291460
  17.1 17.6 %collective-permute-start.6 = (bf16[1040,128]{1,0:T(8,128)(2,1)S(1)}, bf16[1040,128]{1,0:T(8,128)(2,1)S(1)}, u32[]{:S(2)}, u32[]{:S(2)}) collective-permute-start(bf16[1040,128]{1,0:T(8,128)(2,1)S(1)} %get-tuple-element.47.kvo.refs_4_), channel_id=1, source_target_pairs={{0,16},{4,20},{8,24},{12,28},{16,32},{20,36},{24,40},{28,44},{32,4... | collective-permute-start | bytes 798728 | tf_op jit(solution)/shard_map/ppermute | solution.py:300
  18.6 16.2 %collective-permute-start.5 = (bf16[1040,128]{1,0:T(8,128)(2,1)S(1)}, bf16[1040,128]{1,0:T(8,128)(2,1)S(1)}, u32[]{:S(2)}, u32[]{:S(2)}) collective-permute-start(bf16[1040,128]{1,0:T(8,128)(2,1)S(1)} %get-tuple-element.47.kvo.refs_4_), channel_id=1, source_target_pairs={{0,8},{4,12},{8,16},{12,20},{16,24},{20,28},{24,32},{28,36},{32,40... | collective-permute-start | bytes 798728 | tf_op jit(solution)/shard_map/ppermute | solution.py:300
  26.9 20.0 %collective-permute-start.10 = (bf16[1024,128]{1,0:T(8,128)(2,1)S(1)}, bf16[1024,128]{1,0:T(8,128)(2,1)S(1)}, u32[]{:S(2)}, u32[]{:S(2)}) collective-permute-start(bf16[1024,128]{1,0:T(8,128)(2,1)S(1)} %get-tuple-element.59), channel_id=1, source_target_pairs={{0,248},{4,252},{8,0},{12,4},{16,8},{20,12},{24,16},{28,20},{32,24... | collective-permute-start | bytes 786440 | tf_op jit(solution)/shard_map/ppermute | solution.py:300
  27.0 21.2 %collective-permute-start.11 = (bf16[1024,128]{1,0:T(8,128)(2,1)S(1)}, bf16[1024,128]{1,0:T(8,128)(2,1)S(1)}, u32[]{:S(2)}, u32[]{:S(2)}) collective-permute-start(bf16[1024,128]{1,0:T(8,128)(2,1)S(1)} %get-tuple-element.60), channel_id=1, source_target_pairs={{0,240},{4,244},{8,248},{12,252},{16,0},{20,4},{24,8},{28,12},{32,... | collective-permute-start | bytes 786440 | tf_op jit(solution)/shard_map/ppermute | solution.py:300
  41.2 17.6 %collective-permute-start.8 = (bf16[1024,128]{1,0:T(8,128)(2,1)S(1)}, bf16[1024,128]{1,0:T(8,128)(2,1)S(1)}, u32[]{:S(2)}, u32[]{:S(2)}) collective-permute-start(bf16[1024,128]{1,0:T(8,128)(2,1)S(1)} %get-tuple-element.51), channel_id=1, source_target_pairs={{0,248},{4,252},{8,0},{12,4},{16,8},{20,12},{24,16},{28,20},{32,24... | collective-permute-start | bytes 786440 | tf_op jit(solution)/shard_map/ppermute | solution.py:300
  41.3 21.1 %collective-permute-start.9 = (bf16[1024,128]{1,0:T(8,128)(2,1)S(1)}, bf16[1024,128]{1,0:T(8,128)(2,1)S(1)}, u32[]{:S(2)}, u32[]{:S(2)}) collective-permute-start(bf16[1024,128]{1,0:T(8,128)(2,1)S(1)} %get-tuple-element.52), channel_id=1, source_target_pairs={{0,240},{4,244},{8,248},{12,252},{16,0},{20,4},{24,8},{28,12},{32,... | collective-permute-start | bytes 786440 | tf_op jit(solution)/shard_map/ppermute | solution.py:300
  48.9 17.6 %collective-permute-start.12 = (bf16[512,128]{1,0:T(8,128)(2,1)S(1)}, bf16[512,128]{1,0:T(8,128)(2,1)S(1)}, u32[]{:S(2)}, u32[]{:S(2)}) collective-permute-start(bf16[512,128]{1,0:T(8,128)(2,1)S(1)} %get-tuple-element.62), channel_id=1, source_target_pairs={{0,4},{4,0},{8,12},{12,8},{16,20},{20,16},{24,28},{28,24},{32,36},... | collective-permute-start | bytes 393224 | tf_op jit(solution)/shard_map/ppermute | solution.py:300
  58.7 6.3 %collective-permute-start.7 = (bf16[128,4096]{1,0:T(8,128)(2,1)S(1)}, bf16[128,4096]{1,0:T(8,128)(2,1)S(1)}, u32[]{:S(2)}, u32[]{:S(2)}) collective-permute-start(bf16[128,4096]{1,0:T(8,128)(2,1)S(1)} %get-tuple-element.49), channel_id=1, source_target_pairs={{0,4},{4,0},{8,12},{12,8},{16,20},{20,16},{24,28},{28,24},{32,36},... | collective-permute-start | bytes 3145736 | tf_op jit(solution)/shard_map/ppermute | solution.py:300
  63.0 3.5 %collective-permute-start.13 = (bf16[512,128]{1,0:T(8,128)(2,1)S(1)}, bf16[512,128]{1,0:T(8,128)(2,1)S(1)}, u32[]{:S(2)}, u32[]{:S(2)}) collective-permute-start(bf16[512,128]{1,0:T(8,128)(2,1)S(1)} %get-tuple-element.63), channel_id=1, source_target_pairs={{0,4},{4,0},{8,12},{12,8},{16,20},{20,16},{24,28},{28,24},{32,36},... | collective-permute-start | bytes 393224 | tf_op jit(solution)/shard_map/ppermute | solution.py:300
